TPU v7x, 128 devices: a whole 4x4x4 slice. The times are simulated.
128 devices in a mesh: wide: 32 (over z, y, core), narrow: 4 (over x).
Axes of the slice: x: 4, y: 4, z: 4, core: 2. Of those that a mesh axis runs over, the one named last changes fastest.
Arguments:
- inputs: bfloat16 [256, 32768], P('narrow', 'wide'), may hold values from -6 to 6
- out_grad: bfloat16 [256, 32768], P('narrow', 'wide'), may hold values from -6 to 6
- residues: float32 [256, 16], P('narrow'), may hold values from -4 to 4
- decay: float32 [256, 16], P('narrow'), may hold values from 1e-05 to 0.05
Outputs:
- filter_grad: float32 [256, 32768], P('narrow', 'wide')
- residue_grad: float32 [256, 16], P('narrow')
- log_decay_grad: float32 [256, 16], P('narrow')
All inputs are finite; a program needn't handle non-finite values.
Results may differ from a plain program's by a relative error of at most 0.0003.
Values may be sent and summed in bfloat16 or wider, within the bound.
A program may use at most 64 MiB of HBM per device.

v0:
```python
import math

import jax
import jax.numpy as jnp
from jax import lax
from jax.sharding import PartitionSpec as P

HIGH = lax.Precision.HIGHEST


def split_table(table):
    upper = table.astype(jnp.bfloat16)
    upper_wide = lax.optimization_barrier(upper).astype(jnp.float32)
    lower = (table - upper_wide).astype(jnp.bfloat16)
    return (upper, lower)


def table_mix(data, parts):
    upper, lower = parts
    first = jnp.einsum("cjs,qj->cqs", data, upper, preferred_element_type=jnp.float32)
    return first + jnp.einsum("cjs,qj->cqs", data, lower, preferred_element_type=jnp.float32)


def across_blocks(real_in, cos_one, sin_one, cos_tw, sin_tw):
    cos_parts = split_table(cos_one)
    sin_parts = split_table(sin_one)
    mixed_re = table_mix(real_in, cos_parts)
    mixed_im = -table_mix(real_in, sin_parts)
    twist_re = mixed_re * cos_tw[None] + mixed_im * sin_tw[None]
    twist_im = mixed_im * cos_tw[None] - mixed_re * sin_tw[None]
    return jnp.stack([twist_re, twist_im])


def within_block(stacked, cos_big, sin_big, sign):
    parts, chans, slots, width = stacked.shape
    real_part = stacked[0].reshape(chans * slots, width)
    imag_part = stacked[1].reshape(chans * slots, width)
    out_re = jnp.dot(real_part, cos_big, precision=HIGH) + sign * jnp.dot(
        imag_part, sin_big, precision=HIGH
    )
    out_im = jnp.dot(imag_part, cos_big, precision=HIGH) - sign * jnp.dot(
        real_part, sin_big, precision=HIGH
    )
    return (out_re.reshape(chans, slots, width), out_im.reshape(chans, slots, width))


def twist_tables(freqs, offsets, total):
    angle = (freqs[:, None] * offsets[None, :] % total).astype(jnp.float32) * (
        2.0 * math.pi / total
    )
    return (jnp.cos(angle), jnp.sin(angle))


def modal_local(taps_all, rates_all, lags):
    rows, width = taps_all.shape
    modes = rates_all.shape[1]
    group = math.gcd(rows, 128)
    groups_count = rows // group

    def modal_block(packed):
        taps, rates = packed
        power = jnp.exp(-rates[:, :, None] * lags[None, None, :])
        plain_part = jnp.einsum("cb,cnb->cn", taps, power, precision=HIGH)
        weighted_part = jnp.einsum("cb,cnb->cn", taps * lags[None, :], power, precision=HIGH)
        return (plain_part, weighted_part)

    plain_sum, weighted_sum = lax.map(
        modal_block,
        (
            taps_all.reshape(groups_count, group, width),
            rates_all.reshape(groups_count, group, modes),
        ),
    )
    return (plain_sum.reshape(rows, modes), weighted_sum.reshape(rows, modes))


def local(inputs, out_grad, residues, decay):
    chans, block = inputs.shape
    count = lax.axis_size("wide")
    rank = lax.axis_index("wide")
    piece = block // count
    total = 2 * count * block
    scale = 1.0 / math.sqrt(count * block)
    two_pi = 2.0 * math.pi
    slot_ids = jnp.arange(2 * count, dtype=jnp.int32)
    half_ids = slot_ids // 2
    freq_one = jnp.where(
        slot_ids % 2 == 0, half_ids, jnp.where(half_ids == 0, count, 2 * count - half_ids)
    )
    block_ids = jnp.arange(count, dtype=jnp.int32)
    angle_one = (freq_one[:, None] * block_ids[None, :] % (2 * count)).astype(jnp.float32) * (
        two_pi / (2 * count)
    )
    cos_one = jnp.cos(angle_one)
    sin_one = jnp.sin(angle_one)
    full_ids = jnp.arange(block, dtype=jnp.int32)
    angle_big = (full_ids[:, None] * full_ids[None, :] % block).astype(jnp.float32) * (
        two_pi / block
    )
    cos_big = jnp.cos(angle_big)
    sin_big = jnp.sin(angle_big)
    offsets = rank * piece + jnp.arange(piece, dtype=jnp.int32)
    cos_tw, sin_tw = twist_tables(freq_one, offsets, total)
    moved_in, moved_grad = (
        lax.all_to_all(inputs, "wide", split_axis=1, concat_axis=1, tiled=True),
        lax.all_to_all(out_grad, "wide", split_axis=1, concat_axis=1, tiled=True),
    )
    signal = moved_in.reshape(chans, count, piece)
    grad_sig = moved_grad.reshape(chans, count, piece)
    first_sig = across_blocks(signal, cos_one, sin_one, cos_tw, sin_tw)
    second_sig = across_blocks(grad_sig, cos_one, sin_one, cos_tw, sin_tw)
    first_sig, second_sig = (
        lax.all_to_all(first_sig, "wide", split_axis=2, concat_axis=3, tiled=True),
        lax.all_to_all(second_sig, "wide", split_axis=2, concat_axis=3, tiled=True),
    )
    spec_re, spec_im = within_block(first_sig, cos_big, sin_big, 1.0)
    grad_re, grad_im = within_block(second_sig, cos_big, sin_big, 1.0)
    cross_re = grad_re * spec_re + grad_im * spec_im
    cross_im = grad_im * spec_re - grad_re * spec_im
    inv_re, inv_im = within_block(jnp.stack([cross_re, cross_im]), cos_big, sin_big, -1.0)
    own_freq = lax.dynamic_slice_in_dim(freq_one, 2 * rank, 2)
    cos_own, sin_own = twist_tables(own_freq, full_ids, total)
    cos_back = cos_own[None]
    sin_back = sin_own[None]
    turned = jnp.stack(
        [inv_re * cos_back - inv_im * sin_back, inv_im * cos_back + inv_re * sin_back]
    )
    turned = lax.all_to_all(turned, "wide", split_axis=3, concat_axis=2, tiled=True)
    lag_parts = jnp.einsum("cqs,qj->cjs", turned[0], cos_one, precision=HIGH) - jnp.einsum(
        "cqs,qj->cjs", turned[1], sin_one, precision=HIGH
    )
    lag_parts = lag_parts * (scale / total)
    filter_grad = lax.all_to_all(
        lag_parts, "wide", split_axis=1, concat_axis=2, tiled=True
    ).reshape(chans, block)
    lags = (rank * block + full_ids).astype(jnp.float32)
    plain_part, weighted_part = modal_local(filter_grad, decay, lags)
    plain_sum, weighted_sum = lax.psum((plain_part, weighted_part), "wide")
    residue_grad = scale * plain_sum
    log_decay_grad = -scale * decay * residues * weighted_sum
    return (filter_grad, residue_grad, log_decay_grad)


def solution(mesh):
    placed = (P("narrow", "wide"), P("narrow", "wide"), P("narrow", None), P("narrow", None))
    return jax.shard_map(
        local,
        mesh=mesh,
        in_specs=placed,
        out_specs=(P("narrow", "wide"), P("narrow", None), P("narrow", None)),
        check_vma=False,
    )
```

profile of v0, /device:TPU:0, one launch (start us, length us, event | category | flops | bytes accessed | tf_op | source)
XLA Modules:
  0.0 505.4 jit_solution(14839342648925121552)
XLA Ops:
  2.6 8.4 %all-to-all-start.2 = ((bf16[32,2,1024]{2,1,0:T(2,128)(2,1)}), bf16[32,2,1024]{2,1,0:T(2,128)(2,1)S(1)}, u32[]{:S(2)}, u32[]{:S(2)}) async-start(bf16[32,2,1024]{2,1,0:T(2,128)(2,1)} %reshape.273), calls=%async_computation.2 | async-start | bytes 262144 | tf_op jit(solution)/shard_map/all_to_all | solution.py:105
  13.1 5.7 %all-to-all-done.2 = bf16[32,2,1024]{2,1,0:T(2,128)(2,1)S(1)} async-done(((bf16[32,2,1024]{2,1,0:T(2,128)(2,1)}), bf16[32,2,1024]{2,1,0:T(2,128)(2,1)S(1)}, u32[]{:S(2)}, u32[]{:S(2)}) %all-to-all-start.2) | async-done | bytes 131104 | tf_op jit(solution)/shard_map/all_to_all | solution.py:105
  23.7 6.8 %all-to-all-done = bf16[32,2,1024]{2,1,0:T(2,128)(2,1)S(1)} async-done(((bf16[32,2,1024]{2,1,0:T(2,128)(2,1)}), bf16[32,2,1024]{2,1,0:T(2,128)(2,1)S(1)}, u32[]{:S(2)}, u32[]{:S(2)}) %all-to-all-start) | async-done | bytes 131104 | tf_op jit(solution)/shard_map/all_to_all | solution.py:106
  48.4 11.9 %all-to-all-done.3 = f32[32,1,8192]{2,1,0:T(1,128)S(1)} async-done(((f32[32,1,8192]{2,1,0:T(1,128)}), f32[32,1,8192]{2,1,0:T(1,128)S(1)}, u32[]{:S(2)}, u32[]{:S(2)}) %all-to-all-start.3) | async-done | bytes 1048608 | tf_op jit(solution)/shard_map/all_to_all | solution.py:113
  60.4 4.9 all-to-all-start.1
  65.8 4.4 reduce.4
  71.1 4.5 copy.88
  82.2 18.3 %fusion.16 = f32[128,1024]{1,0:T(8,128)S(1)} fusion(f32[128,1024]{1,0:T(8,128)S(1)} %reshape_squeeze.14), kind=kOutput, calls=%fused_computation.20 | convolution fusion | flops 1625292800 | bytes 1048576 | tf_op jit(solution)/shard_map/dot_general | solution.py:38
  101.4 19.1 %fusion.12 = f32[128,1024]{1,0:T(8,128)} fusion(f32[128,1024]{1,0:T(8,128)S(1)} %reshape_squeeze.15), kind=kOutput, calls=%fused_computation.18 | convolution fusion | flops 1625292800 | bytes 1048576 | tf_op jit(solution)/shard_map/dot_general | solution.py:41
  120.5 18.9 %fusion.39 = f32[128,1024]{1,0:T(8,128)} fusion(f32[128,1024]{1,0:T(8,128)S(1)} %fusion.16, f32[128,1024]{1,0:T(8,128)S(1)} %reshape_squeeze.15), kind=kOutput, calls=%fused_computation.38 | convolution fusion | flops 1625423872 | bytes 1572864 | tf_op jit(solution)/shard_map/dot_general | solution.py:38
  139.4 4.5 reduce.5
  144.7 4.5 copy.81
  155.8 18.7 %fusion.14 = f32[128,1024]{1,0:T(8,128)} fusion(f32[128,1024]{1,0:T(8,128)S(1)} %reshape_squeeze.13), kind=kOutput, calls=%fused_computation.19 | convolution fusion | flops 1625292800 | bytes 1048576 | tf_op jit(solution)/shard_map/dot_general | solution.py:41
  175.4 18.5 %fusion.18 = f32[128,1024]{1,0:T(8,128)S(1)} fusion(f32[128,1024]{1,0:T(8,128)S(1)} %reshape_squeeze.12), kind=kOutput, calls=%fused_computation.21 | convolution fusion | flops 1625292800 | bytes 1048576 | tf_op jit(solution)/shard_map/dot_general | solution.py:38
  194.0 18.3 %fusion.42 = f32[128,1024]{1,0:T(8,128)S(1)} fusion(f32[128,1024]{1,0:T(8,128)S(1)} %copy-done.8, f32[128,1024]{1,0:T(8,128)S(1)} %reshape_squeeze.12), kind=kOutput, calls=%fused_computation.39 | convolution fusion | flops 1625423872 | bytes 1572864 | tf_op jit(solution)/shard_map/dot_general | solution.py:41
  212.3 18.7 %fusion.45 = f32[128,1024]{1,0:T(8,128)S(1)} fusion(f32[128,1024]{1,0:T(8,128)S(1)} %copy-done.7, f32[128,1024]{1,0:T(8,128)S(1)} %copy-done.2), kind=kOutput, calls=%fused_computation.40 | convolution fusion | flops 1625423872 | bytes 1572864 | tf_op jit(solution)/shard_map/dot_general | solution.py:41
  231.0 18.4 %multiply_subtract_fusion.1 = (f32[128,1024]{1,0:T(8,128)S(1)}, f32[128,1024]{1,0:T(8,128)S(1)}) fusion(f32[128,1024]{1,0:T(8,128)S(1)} %fusion.45, f32[128,1024]{1,0:T(8,128)S(1)} %fusion.42, f32[128,1024]{1,0:T(8,128)S(1)} %copy-done.6, f32[128,1024]{1,0:T(8,128)S(1)} %fusion.18, f32[128,1024]{1,0:T(8,128)S(1)} %reshape_squeeze.13), kind=kOutput, calls=%fused_computation.55 | convolution fusion | flops 1626210304 | bytes 3670016 | tf_op jit(solution)/shard_map/dot_general | solution.py:38
  249.4 18.4 %fusion.48 = f32[128,1024]{1,0:T(8,128)S(1)} fusion(f32[128,1024]{1,0:T(8,128)S(1)} %get-tuple-element.47), kind=kOutput, calls=%fused_computation.41 | convolution fusion | flops 1625423872 | bytes 1048576 | tf_op jit(solution)/shard_map/dot_general | solution.py:38
  267.9 18.3 %fusion.51 = f32[128,1024]{1,0:T(8,128)S(1)} fusion(f32[128,1024]{1,0:T(8,128)S(1)} %get-tuple-element.48), kind=kOutput, calls=%fused_computation.42 | convolution fusion | flops 1625423872 | bytes 1048576 | tf_op jit(solution)/shard_map/dot_general | solution.py:41
  286.2 18.4 %fusion.54 = f32[128,1024]{1,0:T(8,128)S(1)} fusion(f32[128,1024]{1,0:T(8,128)S(1)} %fusion.48, f32[128,1024]{1,0:T(8,128)S(1)} %get-tuple-element.48), kind=kOutput, calls=%fused_computation.43 | convolution fusion | flops 1625423872 | bytes 1572864 | tf_op jit(solution)/shard_map/dot_general | solution.py:38
  304.9 18.2 %fusion.57 = f32[128,1024]{1,0:T(8,128)S(1)} fusion(f32[128,1024]{1,0:T(8,128)S(1)} %fusion.51, f32[128,1024]{1,0:T(8,128)S(1)} %get-tuple-element.47), kind=kOutput, calls=%fused_computation.44 | convolution fusion | flops 1625423872 | bytes 1572864 | tf_op jit(solution)/shard_map/dot_general | solution.py:41
  327.8 24.6 %all_to_all.72 = f32[32,1,8192]{2,1,0:T(1,128)S(1)} all-to-all(f32[32,1,8192]{2,1,0:T(1,128)S(1)} %reshape.277), channel_id=1, replica_groups=mesh['wide'=32,'narrow'=4] {'wide'}, dimensions={0} | all-to-all | bytes 2097152 | tf_op jit(solution)/shard_map/all_to_all | solution.py:128
  365.8 8.8 %all-to-all-done.5 = f32[32,1,2048]{2,1,0:T(1,128)S(1)} async-done(((f32[32,1,2048]{2,1,0:T(1,128)}), f32[32,1,2048]{2,1,0:T(1,128)S(1)}, u32[]{:S(2)}, u32[]{:S(2)}) %all-to-all-start.5) | async-done | bytes 262176 | tf_op jit(solution)/shard_map/all_to_all | solution.py:133
  378.1 125.6 %all-reduce = (f32[64,16]{0,1:T(8,128)S(1)}, f32[64,16]{0,1:T(8,128)S(1)}) all-reduce(f32[64,16]{0,1:T(8,128)S(1)} %copy.106, f32[64,16]{0,1:T(8,128)S(1)} %copy.111), channel_id=1, replica_groups=mesh['wide'=32,'narrow'=4] {'wide'}, use_global_device_ids=true, to_apply=%region_0.1 | all-reduce | flops 2048 | bytes 16384 | tf_op jit(solution)/shard_map/psum | solution.py:138
  (84 shorter events, 67.1 us)
Async XLA Ops:
  2.6 16.2 %all-to-all-start.2 = ((bf16[32,2,1024]{2,1,0:T(2,128)(2,1)}), bf16[32,2,1024]{2,1,0:T(2,128)(2,1)S(1)}, u32[]{:S(2)}, u32[]{:S(2)}) async-start(bf16[32,2,1024]{2,1,0:T(2,128)(2,1)} %reshape.273), calls=%async_computation.2 | async-start | bytes 262144 | tf_op jit(solution)/shard_map/all_to_all | solution.py:105
  18.8 11.7 %all-to-all-start = ((bf16[32,2,1024]{2,1,0:T(2,128)(2,1)}), bf16[32,2,1024]{2,1,0:T(2,128)(2,1)S(1)}, u32[]{:S(2)}, u32[]{:S(2)}) async-start(bf16[32,2,1024]{2,1,0:T(2,128)(2,1)} %reshape.269), calls=%async_computation | async-start | bytes 262144 | tf_op jit(solution)/shard_map/all_to_all | solution.py:106
  39.1 21.3 %all-to-all-start.3 = ((f32[32,1,8192]{2,1,0:T(1,128)}), f32[32,1,8192]{2,1,0:T(1,128)S(1)}, u32[]{:S(2)}, u32[]{:S(2)}) async-start(f32[32,1,8192]{2,1,0:T(1,128)} %reshape.275), calls=%async_computation.3 | async-start | bytes 2097152 | tf_op jit(solution)/shard_map/all_to_all | solution.py:113
  60.4 4.9 copy-start
  60.4 79.0 %all-to-all-start.1 = ((f32[32,1,8192]{2,1,0:T(1,128)}), f32[32,1,8192]{2,1,0:T(1,128)}, u32[]{:S(2)}, u32[]{:S(2)}) async-start(f32[32,1,8192]{2,1,0:T(1,128)} %reshape.271), calls=%async_computation.1 | async-start | bytes 2097152 | tf_op jit(solution)/shard_map/all_to_all | solution.py:114
  82.2 18.3 %copy-start.1 = (f32[128,1024]{1,0:T(8,128)}, f32[128,1024]{1,0:T(8,128)S(1)}, u32[]{:S(2)}) copy-start(f32[128,1024]{1,0:T(8,128)S(1)} %reshape_squeeze.14) | copy-start | bytes 1572868
  175.4 18.5 %copy-start.8 = (f32[128,1024]{1,0:T(8,128)S(1)}, f32[128,1024]{1,0:T(8,128)}, u32[]{:S(2)}) copy-start(f32[128,1024]{1,0:T(8,128)} %fusion.14) | copy-start | bytes 1572868
  193.9 18.3 %copy-start.2 = (f32[128,1024]{1,0:T(8,128)S(1)}, f32[128,1024]{1,0:T(8,128)}, u32[]{:S(2)}) copy-start(f32[128,1024]{1,0:T(8,128)} %copy-done.1) | copy-start | bytes 1572868
  193.9 18.3 %copy-start.7 = (f32[128,1024]{1,0:T(8,128)S(1)}, f32[128,1024]{1,0:T(8,128)}, u32[]{:S(2)}) copy-start(f32[128,1024]{1,0:T(8,128)} %fusion.12) | copy-start | bytes 1572868
  212.3 18.7 %copy-start.6 = (f32[128,1024]{1,0:T(8,128)S(1)}, f32[128,1024]{1,0:T(8,128)}, u32[]{:S(2)}) copy-start(f32[128,1024]{1,0:T(8,128)} %fusion.39) | copy-start | bytes 1572868
  357.5 8.2 %copy-start.4 = (f32[64,16]{0,1:T(8,128)S(1)}, f32[64,16]{0,1:T(8,128)}, u32[]{:S(2)}) copy-start(f32[64,16]{0,1:T(8,128)} %param.7) | copy-start | bytes 12292
  360.2 144.1 %copy-start.5 = (f32[64,16]{0,1:T(8,128)S(1)}, f32[64,16]{0,1:T(8,128)}, u32[]{:S(2)}) copy-start(f32[64,16]{0,1:T(8,128)} %param.6) | copy-start | bytes 12292
  361.5 13.1 %all-to-all-start.5 = ((f32[32,1,2048]{2,1,0:T(1,128)}), f32[32,1,2048]{2,1,0:T(1,128)S(1)}, u32[]{:S(2)}, u32[]{:S(2)}) async-start(f32[32,1,2048]{2,1,0:T(1,128)} %reshape.279), calls=%async_computation.5 | async-start | bytes 524288 | tf_op jit(solution)/shard_map/all_to_all | solution.py:133
  376.7 128.2 %copy-start.3 = (f32[64,1024]{1,0:T(8,128)}, f32[64,1024]{1,0:T(8,128)S(1)}, u32[]{:S(2)}) copy-start(f32[64,1024]{1,0:T(8,128)S(1)} %copy.101) | copy-start | bytes 786436
where the time goes:
time: 514 us; the launch traced here: 505 us
  matrix products  228 us (44%)
  blocking collectives  150 us (29%)
  local copies, waits for them, and re-layouts  47.8 us (9%)
  waiting for transfers between devices  33.1 us (6%)
  starting transfers between devices  25.2 us (5%)
  other arithmetic  18.9 us (4%)
    psum x1, blocking collectives, local(): plain_sum, weighted_sum = lax.psum((plain_part, weighted_part), 'wide')  126 us
    dot_general x3, matrix products, within_block(): jnp.dot(imag_part, cos_big, precision=HIGH)  55.9 us
    dot_general x3, matrix products, within_block(): jnp.dot(imag_part, sin_big, precision=HIGH)  55.7 us
    dot_general x3, matrix products, within_block(): jnp.dot(real_part, sin_big, precision=HIGH)  55.3 us
    dot_general x3, matrix products, within_block(): jnp.dot(real_part, cos_big, precision=HIGH)  55.2 us
    all_to_all x1, blocking collectives, local(): lax.all_to_all(turned, 'wide', split_axis=3, concat_axis=2, tiled=True)  24.6 us
    unnamed x34, local copies, waits for them, and re-layouts  15.9 us
    all_to_all x1, waiting for transfers between devices, local(): lax.all_to_all(first_sig, 'wide', split_axis=2, concat_axis=3, tiled=True)  11.9 us
  transfers between devices with their start and end apart: 5, of which 4 were waited for; matrix products, arithmetic and copies ran while one was open for 16% of the time, Pallas kernels for 0%

commit v1 on v0

v1 whole, which is shorter than its diff:
```python
import math

import jax
import jax.numpy as jnp
from jax import lax
from jax.experimental import pallas as pl
from jax.experimental.pallas import tpu as pltpu
from jax.sharding import PartitionSpec as P

F32 = jnp.float32
BF16 = jnp.bfloat16
MESH = pl.DeviceIdType.MESH

LANES = 128
SHIFTS = 32
TURNS = LANES // SHIFTS


def to_rows(block_ref, stage, send):
    chans, width = block_ref.shape
    tiles = width // LANES
    for k in range(tiles):
        stage[pl.ds(k, chans, stride=tiles), :] = block_ref[:, k * LANES : (k + 1) * LANES].astype(F32)
    send[...] = stage[...].astype(BF16)


def build_toeplitz(ch, signal, toep):
    row = lax.broadcasted_iota(jnp.int32, (SHIFTS, LANES), 0)
    lane = lax.broadcasted_iota(jnp.int32, (SHIFTS, LANES), 1)
    keep = lane >= row

    def step(i, before):
        for p in range(2):
            for q in range(8):
                m = 16 * i + 8 * p + q
                spread = jnp.broadcast_to(signal[ch, pl.ds(m, 1), :], (SHIFTS, LANES))
                now = pltpu.roll(spread, 0, 1, stride=1, stride_axis=0)
                toep[ch, i, q * SHIFTS : (q + 1) * SHIFTS, p * LANES : (p + 1) * LANES] = jnp.where(
                    keep, now, before
                ).astype(BF16)
                before = now
        return before

    lax.fori_loop(0, 16, step, jnp.zeros((SHIFTS, LANES), F32))


def build_shifted(ch, grad, shifted):
    lane = lax.broadcasted_iota(jnp.int32, (264, LANES), 1)
    here = grad[ch, 0:264, :]
    after = grad[ch, 1:265, :]
    for h in range(TURNS):
        moved = here
        if h:
            moved = pltpu.roll(jnp.where(lane < SHIFTS * h, after, here), LANES - SHIFTS * h, 1)
        shifted[ch, h] = jnp.concatenate([moved[0:256], moved[8:264]], axis=1).astype(BF16)


def correlate(ch, toep, shifted, acc, scale):
    acc[...] = jnp.zeros_like(acc)
    for i in range(16):
        live = 256 - 16 * i
        table = toep[ch, i]
        for h in range(TURNS):
            part = lax.dot_general(
                shifted[ch, h, 16 * i : 256, :],
                table,
                (((1,), (1,)), ((), ())),
                preferred_element_type=F32,
            )
            acc[h, 0, 0:live] += part[:, :LANES]
            acc[h, 1, 0:live] += part[:, LANES:]
    group = lax.broadcasted_iota(jnp.int32, (256, LANES), 1) // SHIFTS
    total = None
    for turn in range(TURNS):
        mixed = None
        for low in range(TURNS):
            h = (low + turn) % TURNS
            term = acc[h, 0, low : low + 256, :] + acc[h, 1, low + 4 : low + 260, :]
            mixed = term if mixed is None else jnp.where(group == low, term, mixed)
        if turn:
            mixed = pltpu.roll(mixed, SHIFTS * turn, 1)
        total = mixed if total is None else total + mixed
    return total * scale


def kernel(
    x_ref, g_ref, res_ref, dec_ref, out_ref, rg_ref, ld_ref,
    stage, send_x, send_g, recv_x, recv_g, signal, grad, toep, shifted, acc,
    send_c, recv_c, fine, coarse, send_m, recv_m,
    ssem_in, rsem_in, ssem_c, rsem_c, ssem_m, rsem_m,
):
    count = lax.axis_size("wide")
    me = lax.axis_index("wide")
    seq = count * x_ref.shape[1]
    scale = 1.0 / math.sqrt(seq)

    barrier = pltpu.get_barrier_semaphore()

    @pl.loop(1, count)
    def _(k):
        pl.semaphore_signal(
            barrier, inc=1, device_id={"wide": lax.rem(me + k, count)}, device_id_type=MESH
        )

    to_rows(x_ref, stage, send_x)
    to_rows(g_ref, stage, send_g)
    pl.semaphore_wait(barrier, count - 1)

    def moved(which, send, recv, to, at):
        return pltpu.make_async_remote_copy(
            src_ref=send.at[pl.ds(pl.multiple_of(16 * to, 16), 16), :],
            dst_ref=recv.at[pl.ds(pl.multiple_of(16 * at, 16), 16), :],
            send_sem=ssem_in.at[which, to],
            recv_sem=rsem_in.at[which, at],
            device_id={"wide": to},
            device_id_type=MESH,
        )

    @pl.loop(1, count)
    def _(k):
        moved(0, send_x, recv_x, lax.rem(me + k, count), me).start()

    @pl.loop(1, count)
    def _(k):
        moved(1, send_g, recv_g, lax.rem(me + k, count), me).start()

    mine = pl.ds(pl.multiple_of(16 * me, 16), 16)
    recv_x[mine, :] = send_x[mine, :]
    recv_g[mine, :] = send_g[mine, :]

    lane_big = lax.broadcasted_iota(jnp.int32, (256, LANES), 1)
    block_at = (lax.broadcasted_iota(jnp.int32, (256, LANES), 0) * LANES).astype(F32)
    lane_small = lax.broadcasted_iota(jnp.int32, (LANES, LANES), 1)
    offset_at = lax.broadcasted_iota(jnp.int32, (LANES, LANES), 0).astype(F32)
    rates = []
    for ch in range(2):
        rate = dec_ref[pl.ds(2 * me + ch, 1), :]
        rate = jnp.concatenate([rate] * 8, axis=1)
        rates.append(rate)
        power = jnp.exp(-rate * offset_at)
        weighted = jnp.logical_and(lane_small >= 16, lane_small < 32)
        fine[ch] = jnp.where(lane_small < 48, jnp.where(weighted, offset_at * power, power), 0.0)
        power = jnp.exp(-rate * block_at)
        coarse[ch] = jnp.where(lane_big < 32, power, block_at * power)

    @pl.loop(1, count)
    def _(k):
        at = lax.rem(me + k, count)
        moved(0, send_x, recv_x, at, at).wait_recv()

    wide = recv_x[...].astype(F32).reshape(32, 16, LANES)
    for ch in range(2):
        signal[ch] = wide[:, 8 * ch : 8 * ch + 8].reshape(256, LANES)
    for ch in range(2):
        build_toeplitz(ch, signal, toep)

    @pl.loop(1, count)
    def _(k):
        at = lax.rem(me + k, count)
        moved(1, send_g, recv_g, at, at).wait_recv()

    wide = recv_g[...].astype(F32).reshape(32, 16, LANES)
    for ch in range(2):
        grad[ch, 0:256] = wide[:, 8 * ch : 8 * ch + 8].reshape(256, LANES)
        grad[ch, 256:] = jnp.zeros((16, LANES), F32)
        build_shifted(ch, grad, shifted)

    def lags_to(ch, to, at):
        return pltpu.make_async_remote_copy(
            src_ref=send_c.at[ch, pl.ds(pl.multiple_of(8 * to, 8), 8), :],
            dst_ref=recv_c.at[pl.ds(pl.multiple_of(16 * at + 8 * ch, 8), 8), :],
            send_sem=ssem_c.at[ch, to],
            recv_sem=rsem_c.at[ch, at],
            device_id={"wide": to},
            device_id_type=MESH,
        )

    for ch in range(2):
        send_c[ch] = correlate(ch, toep, shifted, acc, scale)

        @pl.loop(1, count)
        def _(k):
            lags_to(ch, lax.rem(me + k, count), me).start()

        recv_c[pl.ds(pl.multiple_of(16 * me + 8 * ch, 8), 8), :] = send_c[
            ch, pl.ds(pl.multiple_of(8 * me, 8), 8), :
        ]

    lane_row = lax.broadcasted_iota(jnp.int32, (1, LANES), 1)
    sub = lax.broadcasted_iota(jnp.int32, (8, LANES), 0)
    tile = jnp.zeros((8, LANES), F32)
    for ch in range(2):
        part = jnp.dot(
            send_c[ch], fine[ch], precision=lax.Precision.HIGHEST, preferred_element_type=F32
        )
        sums = jnp.sum(part * coarse[ch], axis=0, keepdims=True)
        both = sums + pltpu.roll(sums, LANES - 16, 1)
        residue = jnp.concatenate([res_ref[pl.ds(2 * me + ch, 1), :]] * 8, axis=1)
        line = jnp.where(lane_row < 16, scale * sums, -scale * rates[ch] * residue * both)
        tile = tile + jnp.where(sub == 2 * lax.rem(me, 4) + ch, line, 0.0)
    send_m[...] = tile
    own = pl.ds(pl.multiple_of(8 * me, 8), 8)
    recv_m[own, :] = tile

    def modes_to(to, at):
        return pltpu.make_async_remote_copy(
            src_ref=send_m,
            dst_ref=recv_m.at[pl.ds(pl.multiple_of(8 * at, 8), 8), :],
            send_sem=ssem_m.at[to],
            recv_sem=rsem_m.at[at],
            device_id={"wide": to},
            device_id_type=MESH,
        )

    @pl.loop(1, count)
    def _(k):
        modes_to(lax.rem(me + k, count), me).start()

    @pl.loop(1, count)
    def _(k):
        at = lax.rem(me + k, count)
        for ch in range(2):
            lags_to(ch, at, at).wait_recv()

    chans = out_ref.shape[0]
    for k in range(8):
        out_ref[:, k * LANES : (k + 1) * LANES] = recv_c[pl.ds(k, chans, stride=8), :]

    @pl.loop(1, count)
    def _(k):
        at = lax.rem(me + k, count)
        modes_to(at, at).wait_recv()

    tiles = recv_m[...].reshape(8, 4, 8, LANES)
    rows = (tiles[:, 0] + tiles[:, 1] + tiles[:, 2] + tiles[:, 3]).reshape(64, LANES)
    rg_ref[...] = rows[:, 0:16]
    ld_ref[...] = rows[:, 16:32]

    @pl.loop(1, count)
    def _(k):
        to = lax.rem(me + k, count)
        moved(0, send_x, recv_x, to, me).wait_send()
        moved(1, send_g, recv_g, to, me).wait_send()
        for ch in range(2):
            lags_to(ch, to, me).wait_send()
        modes_to(to, me).wait_send()


def local(inputs, out_grad, residues, decay):
    chans, block = inputs.shape
    count = lax.axis_size("wide")
    vmem = pl.BlockSpec(memory_space=pltpu.VMEM)
    dma = pltpu.SemaphoreType.DMA
    return pl.pallas_call(
        kernel,
        out_shape=(
            jax.ShapeDtypeStruct((chans, block), F32),
            jax.ShapeDtypeStruct(residues.shape, F32),
            jax.ShapeDtypeStruct(decay.shape, F32),
        ),
        in_specs=[vmem] * 4,
        out_specs=(vmem,) * 3,
        scratch_shapes=[
            pltpu.VMEM((512, LANES), F32),
            pltpu.VMEM((512, LANES), BF16),
            pltpu.VMEM((512, LANES), BF16),
            pltpu.VMEM((512, LANES), BF16),
            pltpu.VMEM((512, LANES), BF16),
            pltpu.VMEM((2, 256, LANES), F32),
            pltpu.VMEM((2, 272, LANES), F32),
            pltpu.VMEM((2, 16, 256, 256), BF16),
            pltpu.VMEM((2, TURNS, 256, 256), BF16),
            pltpu.VMEM((TURNS, 2, 264, LANES), F32),
            pltpu.VMEM((2, 256, LANES), F32),
            pltpu.VMEM((512, LANES), F32),
            pltpu.VMEM((2, LANES, LANES), F32),
            pltpu.VMEM((2, 256, LANES), F32),
            pltpu.VMEM((8, LANES), F32),
            pltpu.VMEM((256, LANES), F32),
            dma((2, count)),
            dma((2, count)),
            dma((2, count)),
            dma((2, count)),
            dma((count,)),
            dma((count,)),
        ],
        compiler_params=pltpu.CompilerParams(
            collective_id=0, has_side_effects=True, vmem_limit_bytes=32 * 2**20
        ),
    )(inputs, out_grad, residues, decay)


def solution(mesh):
    placed = (P("narrow", "wide"), P("narrow", "wide"), P("narrow", None), P("narrow", None))
    return jax.shard_map(
        local,
        mesh=mesh,
        in_specs=placed,
        out_specs=(P("narrow", "wide"), P("narrow", None), P("narrow", None)),
        check_vma=False,
    )
```

time: 514 us -> 38 us (0.07)
  the two profiles are of different devices: /device:TPU:0 before, /device:TPU:1 now
where the time goes in v1:
time: 38 us; the launch traced here: 37.8 us
  Pallas kernels  32.5 us (86%)
  local copies, waits for them, and re-layouts  4.72 us (12%)
  between operations  0.65 us (2%)
    pallas_call x1, Pallas kernels, local(): pl.pallas_call(kernel, out_shape=(jax.ShapeDtypeStruct((chans, block), F3...  32.5 us
    unnamed x9, local copies, waits for them, and re-layouts  3.38 us
    pallas_call x2, local copies, waits for them, and re-layouts, local(): pl.pallas_call(kernel, out_shape=(jax.ShapeDtypeStruct((chans, block), F3...  1.34 us

profile of v1, /device:TPU:1, one launch (start us, length us, event | category | flops | bytes accessed | tf_op | source)
XLA Modules:
  0.0 37.8 jit_solution(16289250028484576549)
XLA Ops:
  0.6 0.0 copy-start.2
  0.6 0.8 %copy.7.res_ref = f32[64,16]{1,0:T(8,128)S(1)} copy(f32[64,16]{0,1:T(8,128)} %param.6) | data formatting | bytes 8192 | tf_op args[2]
  1.4 0.0 copy-done.2
  1.4 0.1 copy.8.dec_ref
  1.5 0.0 copy-start
  1.5 0.9 %copy-done = bf16[64,1024]{1,0:T(8,128)(2,1)S(1)} copy-done((bf16[64,1024]{1,0:T(8,128)(2,1)S(1)}, bf16[64,1024]{1,0:T(8,128)(2,1)}, u32[]{:S(2)}) %copy-start) | copy-done | bytes 131096
  2.4 0.0 copy-start.1
  2.4 0.9 %copy-done.1 = bf16[64,1024]{1,0:T(8,128)(2,1)S(1)} copy-done((bf16[64,1024]{1,0:T(8,128)(2,1)S(1)}, bf16[64,1024]{1,0:T(8,128)(2,1)}, u32[]{:S(2)}) %copy-start.1) | copy-done | bytes 131096
  3.3 32.5 %shard_map.67 = (f32[64,1024]{1,0:T(8,128)S(1)}, f32[64,16]{1,0:T(8,128)S(1)}, f32[64,16]{1,0:T(8,128)S(1)}) custom-call(bf16[64,1024]{1,0:T(8,128)(2,1)S(1)} %copy-done, bf16[64,1024]{1,0:T(8,128)(2,1)S(1)} %copy-done.1, f32[64,16]{1,0:T(8,128)S(1)} %copy.7.res_ref, f32[64,16]{1,0:T(8,128)S(1)} %copy.8.dec_ref), custom_call_target="tpu_custom_call" | custom-call | tf_op jit(solution)/shard_map/pallas_call | solution.py:254
  35.8 0.7 %copy.9 = f32[64,16]{0,1:T(8,128)} copy(f32[64,16]{1,0:T(8,128)S(1)} %get-tuple-element.4) | data formatting | bytes 8192 | tf_op jit(solution)/shard_map/pallas_call | solution.py:254
  36.5 0.7 %copy.10 = f32[64,16]{0,1:T(8,128)} copy(f32[64,16]{1,0:T(8,128)S(1)} %get-tuple-element.5) | data formatting | bytes 8192 | tf_op jit(solution)/shard_map/pallas_call | solution.py:254
  37.1 0.7 %copy.12 = f32[64,1024]{1,0:T(8,128)} copy(f32[64,1024]{1,0:T(8,128)S(1)} %get-tuple-element.9) | data formatting | bytes 524288
Async XLA Ops:
  0.6 0.8 %copy-start.2 = (f32[64,16]{0,1:T(8,128)S(1)}, f32[64,16]{0,1:T(8,128)}, u32[]{:S(2)}) copy-start(f32[64,16]{0,1:T(8,128)} %param.7) | copy-start | bytes 12292
  1.5 0.9 %copy-start = (bf16[64,1024]{1,0:T(8,128)(2,1)S(1)}, bf16[64,1024]{1,0:T(8,128)(2,1)}, u32[]{:S(2)}) copy-start(bf16[64,1024]{1,0:T(8,128)(2,1)} %x_ref.1) | copy-start | bytes 393220
  2.4 0.9 %copy-start.1 = (bf16[64,1024]{1,0:T(8,128)(2,1)S(1)}, bf16[64,1024]{1,0:T(8,128)(2,1)}, u32[]{:S(2)}) copy-start(bf16[64,1024]{1,0:T(8,128)(2,1)} %g_ref.1) | copy-start | bytes 393220

commit v2 on v1

v2 whole, which is shorter than its diff:
```python
import math

import jax
import jax.numpy as jnp
from jax import lax
from jax.experimental import pallas as pl
from jax.experimental.pallas import tpu as pltpu
from jax.sharding import PartitionSpec as P

F32 = jnp.float32
BF16 = jnp.bfloat16
MESH = pl.DeviceIdType.MESH

LANES = 128
SHIFTS = 32
TURNS = LANES // SHIFTS
PEERS = 32
RING = (0, 1, 2, 1)
OFFSETS = sorted(
    ((dz, dy, dc) for dz in range(4) for dy in range(4) for dc in range(2) if dz or dy or dc),
    key=lambda o: (-RING[o[0]] - RING[o[1]], -o[2], o),
)


def place(me):
    return me // 8, (me // 2) % 4, me % 2


def shifted_peer(at, dz, dy, dc):
    z, y, core = at
    return ((z + dz) % 4) * 8 + ((y + dy) % 4) * 2 + (core + dc) % 2


def aligned(index, size):
    return pl.ds(pl.multiple_of(index * size, size), size)


def to_rows(block_ref, which, stage):
    for ch in range(2):
        for k in range(8):
            stage[pl.ds(16 * which + 8 * ch + k, PEERS, stride=32), :] = block_ref[
                PEERS * ch : PEERS * (ch + 1), k * LANES : (k + 1) * LANES
            ].astype(F32)


def build_toeplitz(j, recv, toep, tails):
    row = lax.broadcasted_iota(jnp.int32, (SHIFTS, LANES), 0)
    lane = lax.broadcasted_iota(jnp.int32, (SHIFTS, LANES), 1)
    keep = lane >= row
    block = recv[pl.ds(pl.multiple_of(32 * j, 32), 16), :].astype(F32)
    for ch in range(2):
        before = jnp.zeros((SHIFTS, LANES), F32)
        for q in range(8):
            spread = jnp.broadcast_to(block[8 * ch + q : 8 * ch + q + 1], (SHIFTS, LANES))
            now = pltpu.roll(spread, 0, 1, stride=1, stride_axis=0)
            toep[ch, j, q * SHIFTS : (q + 1) * SHIFTS, :] = jnp.where(keep, now, before).astype(BF16)
            before = now
        tails[ch, j] = jnp.where(keep, 0.0, before).astype(BF16)


def build_shifted(ch, grad, shifted):
    lane = lax.broadcasted_iota(jnp.int32, (264, LANES), 1)
    here = grad[ch, 0:264, :]
    after = grad[ch, 1:265, :]
    turns = []
    for h in range(TURNS):
        moved = here
        if h:
            moved = pltpu.roll(jnp.where(lane < SHIFTS * h, after, here), LANES - SHIFTS * h, 1)
        turns.append(jnp.concatenate([moved[0:256], moved[8:264]], axis=1).reshape(32, 8, 256))
    shifted[ch] = jnp.stack(turns, axis=1).reshape(1024, 256).astype(BF16)


def correlate(ch, toep, shifted, acc, scale):
    acc[...] = jnp.zeros_like(acc)
    for i in range(16):
        live = 256 - 16 * i
        table = jnp.concatenate([toep[ch, 2 * i], toep[ch, 2 * i + 1]], axis=1)
        part = lax.dot_general(
            shifted[ch, 64 * i : 1024, :],
            table,
            (((1,), (1,)), ((), ())),
            preferred_element_type=F32,
        ).reshape(live // 8, TURNS, 8, 256)
        for h in range(TURNS):
            own = part[:, h].reshape(live, 256)
            acc[h, 0, 0:live] += own[:, :LANES]
            acc[h, 1, 0:live] += own[:, LANES:]
    group = lax.broadcasted_iota(jnp.int32, (256, LANES), 1) // SHIFTS
    total = None
    for turn in range(TURNS):
        mixed = None
        for low in range(TURNS):
            h = (low + turn) % TURNS
            term = acc[h, 0, low : low + 256, :] + acc[h, 1, low + 4 : low + 260, :]
            mixed = term if mixed is None else jnp.where(group == low, term, mixed)
        if turn:
            mixed = pltpu.roll(mixed, SHIFTS * turn, 1)
        total = mixed if total is None else total + mixed
    return total * scale


def channel_row(ref, channel):
    lane = lax.broadcasted_iota(jnp.int32, ref.shape, 1)
    column = jnp.sum(jnp.where(lane == channel, ref[...], 0.0), axis=1, keepdims=True)
    spread = jnp.broadcast_to(column, (16, LANES))
    sub = lax.broadcasted_iota(jnp.int32, (16, LANES), 0)
    lane = lax.broadcasted_iota(jnp.int32, (16, LANES), 1)
    return jnp.sum(jnp.where(lane % 16 == sub, spread, 0.0), axis=0, keepdims=True)


def exchange(
    x_hbm, g_hbm, res_hbm, dec_hbm, recv_c, recv_m,
    x_ref, g_ref, res_ref, dec_ref, stage, send, recv, grad, toep, tails, shifted, acc,
    send_c, fine, coarse, send_m,
    lsem, ssem_in, rsem_in, ssem_c, rsem_c, ssem_m, rsem_m,
):
    me = lax.axis_index("wide")
    at = place(me)
    peers = [shifted_peer(at, *offset) for offset in OFFSETS]
    scale = 1.0 / math.sqrt(PEERS * x_ref.shape[1])

    barrier = pltpu.get_barrier_semaphore()
    for peer in peers:
        pl.semaphore_signal(barrier, inc=1, device_id={"wide": peer}, device_id_type=MESH)

    fetches = [
        pltpu.make_async_copy(src, dst, lsem.at[n])
        for n, (src, dst) in enumerate(
            ((x_hbm, x_ref), (g_hbm, g_ref), (dec_hbm, dec_ref), (res_hbm, res_ref))
        )
    ]
    for fetch in fetches:
        fetch.start()
    for which, ref in ((0, x_ref), (1, g_ref)):
        fetches[which].wait()
        to_rows(ref, which, stage)
    send[...] = stage[...].astype(BF16)
    pl.semaphore_wait(barrier, PEERS - 1)

    def signals_to(to, source):
        return pltpu.make_async_remote_copy(
            src_ref=send.at[aligned(to, 32), :],
            dst_ref=recv.at[aligned(source, 32), :],
            send_sem=ssem_in.at[to],
            recv_sem=rsem_in.at[source],
            device_id={"wide": to},
            device_id_type=MESH,
        )

    for peer in peers:
        signals_to(peer, me).start()
    recv[aligned(me, 32), :] = send[aligned(me, 32), :]

    fetches[2].wait()
    fetches[3].wait()
    lane_big = lax.broadcasted_iota(jnp.int32, (256, LANES), 1)
    block_at = (lax.broadcasted_iota(jnp.int32, (256, LANES), 0) * LANES).astype(F32)
    lane_small = lax.broadcasted_iota(jnp.int32, (LANES, LANES), 1)
    offset_at = lax.broadcasted_iota(jnp.int32, (LANES, LANES), 0).astype(F32)
    rates = []
    for ch in range(2):
        rate = channel_row(dec_ref, PEERS * ch + me)
        rates.append(rate)
        power = jnp.exp(-rate * offset_at)
        weighted = jnp.logical_and(lane_small >= 16, lane_small < 32)
        fine[ch] = jnp.where(lane_small < 48, jnp.where(weighted, offset_at * power, power), 0.0)
        power = jnp.exp(-rate * block_at)
        coarse[ch] = jnp.where(lane_big < 32, power, block_at * power)

    build_toeplitz(me, recv, toep, tails)

    def arrival(n, carry):
        dy, dz = (n // 2) % 4, n // 8
        dy = dy + (dy // 2) * (1 - 2 * (dy % 2))
        dz = dz + (dz // 2) * (1 - 2 * (dz % 2))
        source = shifted_peer(at, dz, dy, n % 2)
        signals_to(source, source).wait_recv()
        build_toeplitz(source, recv, toep, tails)
        return carry

    lax.fori_loop(1, PEERS, arrival, 0)

    for ch in range(2):
        toep[ch, 1:, 0:SHIFTS, :] = toep[ch, 1:, 0:SHIFTS, :] + tails[ch, : PEERS - 1]
        grad[ch, 0:256] = (
            recv[...].reshape(PEERS, 32, LANES)[:, 16:32].astype(F32)[:, 8 * ch : 8 * ch + 8]
        ).reshape(256, LANES)
        grad[ch, 256:] = jnp.zeros((16, LANES), F32)
        build_shifted(ch, grad, shifted)

    def lags_to(ch, to, source):
        return pltpu.make_async_remote_copy(
            src_ref=send_c.at[ch, aligned(to, 8), :],
            dst_ref=recv_c.at[pl.ds(pl.multiple_of(16 * source + 8 * ch, 8), 8), :],
            send_sem=ssem_c.at[ch, to],
            recv_sem=rsem_c.at[ch, source],
            device_id={"wide": to},
            device_id_type=MESH,
        )

    def modal(ch):
        part = jnp.dot(
            send_c[ch], fine[ch], precision=lax.Precision.HIGHEST, preferred_element_type=F32
        )
        sums = jnp.sum(part * coarse[ch], axis=0, keepdims=True)
        both = sums + pltpu.roll(sums, LANES - 16, 1)
        residue = channel_row(res_ref, PEERS * ch + me)
        lane = lax.broadcasted_iota(jnp.int32, (1, LANES), 1)
        line = jnp.where(lane < 16, scale * sums, -scale * rates[ch] * residue * both)
        return jnp.where(lane < 32, line, 0.0)

    lines = []
    for ch in range(2):
        send_c[ch] = correlate(ch, toep, shifted, acc, scale)
        for peer in peers:
            lags_to(ch, peer, me).start()
        recv_c[pl.ds(pl.multiple_of(16 * me + 8 * ch, 8), 8), :] = send_c[ch, aligned(me, 8), :]
        lines.append(modal(ch))
    line = lines[0] + pltpu.roll(lines[1], 32, 1)
    send_m[...] = line
    recv_m[me] = line

    def modes_to(to, source):
        return pltpu.make_async_remote_copy(
            src_ref=send_m,
            dst_ref=recv_m.at[source],
            send_sem=ssem_m.at[to],
            recv_sem=rsem_m.at[source],
            device_id={"wide": to},
            device_id_type=MESH,
        )

    for peer in peers:
        modes_to(peer, me).start()

    @pl.loop(1, PEERS)
    def _(k):
        peer = (me + k) % PEERS
        signals_to(peer, me).wait_send()
        lags_to(0, peer, me).wait_send()
        lags_to(1, peer, me).wait_send()
        modes_to(peer, me).wait_send()
        lags_to(0, peer, peer).wait_recv()
        lags_to(1, peer, peer).wait_recv()
        modes_to(peer, peer).wait_recv()


def regroup(c_ref, m_ref, out_ref, rg_ref, ld_ref):
    for ch in range(2):
        for k in range(8):
            out_ref[PEERS * ch : PEERS * (ch + 1), k * LANES : (k + 1) * LANES] = c_ref[
                pl.ds(8 * ch + k, PEERS, stride=16), :
            ]
    lines = jnp.transpose(m_ref[:, 0, :])
    rg_ref[...] = jnp.concatenate([lines[0:16], lines[32:48]], axis=1)
    ld_ref[...] = jnp.concatenate([lines[16:32], lines[48:64]], axis=1)


def local(inputs, out_grad, residues, decay):
    chans, block = inputs.shape
    modes = residues.shape[1]
    vmem = pl.BlockSpec(memory_space=pltpu.VMEM)
    hbm = pl.BlockSpec(memory_space=pltpu.HBM)
    dma = pltpu.SemaphoreType.DMA
    lags, lines = pl.pallas_call(
        exchange,
        out_shape=(
            jax.ShapeDtypeStruct((512, LANES), F32),
            jax.ShapeDtypeStruct((PEERS, 1, LANES), F32),
        ),
        in_specs=[hbm] * 4,
        out_specs=(vmem, vmem),
        scratch_shapes=[
            pltpu.VMEM((chans, block), BF16),
            pltpu.VMEM((chans, block), BF16),
            pltpu.VMEM((modes, chans), F32),
            pltpu.VMEM((modes, chans), F32),
            pltpu.VMEM((1024, LANES), F32),
            pltpu.VMEM((1024, LANES), BF16),
            pltpu.VMEM((1024, LANES), BF16),
            pltpu.VMEM((2, 272, LANES), F32),
            pltpu.VMEM((2, PEERS, 256, LANES), BF16),
            pltpu.VMEM((2, PEERS, SHIFTS, LANES), BF16),
            pltpu.VMEM((2, 1024, 256), BF16),
            pltpu.VMEM((TURNS, 2, 264, LANES), F32),
            pltpu.VMEM((2, 256, LANES), F32),
            pltpu.VMEM((2, LANES, LANES), F32),
            pltpu.VMEM((2, 256, LANES), F32),
            pltpu.VMEM((1, LANES), F32),
            dma((4,)),
            dma((PEERS,)),
            dma((PEERS,)),
            dma((2, PEERS)),
            dma((2, PEERS)),
            dma((PEERS,)),
            dma((PEERS,)),
        ],
        compiler_params=pltpu.CompilerParams(
            collective_id=0, has_side_effects=True, vmem_limit_bytes=32 * 2**20
        ),
    )(inputs, out_grad, residues.T, decay.T)
    filter_grad, residue_grad, log_decay_grad = pl.pallas_call(
        regroup,
        out_shape=(
            jax.ShapeDtypeStruct((chans, block), F32),
            jax.ShapeDtypeStruct((modes, chans), F32),
            jax.ShapeDtypeStruct((modes, chans), F32),
        ),
        in_specs=[vmem] * 2,
        out_specs=(vmem,) * 3,
    )(lags, lines)
    return filter_grad, residue_grad.T, log_decay_grad.T


def solution(mesh):
    placed = (P("narrow", "wide"), P("narrow", "wide"), P("narrow", None), P("narrow", None))
    return jax.shard_map(
        local,
        mesh=mesh,
        in_specs=placed,
        out_specs=(P("narrow", "wide"), P("narrow", None), P("narrow", None)),
        check_vma=False,
    )
```

time: 38 us -> 37.2 us (0.979)
  Pallas kernels: 32.5 us -> 31.8 us
    pallas_call x2 -> x0, local copies, waits for them, and re-layouts: 1.34 us -> none  [local(): pl.pallas_call(kernel, out_shape=(jax.ShapeDtypeStruct((chans, block), F3...]
    unnamed x9 -> x12, local copies, waits for them, and re-layouts: 3.38 us -> 4.48 us
    pallas_call x1 -> x2, Pallas kernels: 32.5 us -> 31.8 us  [the longest x1 30 us: local(): pl.pallas_call(exchange, out_shape=(jax.ShapeDtypeStruct((512, LANES), F3...]
where the time goes in v2:
time: 37.2 us; the launch traced here: 36.9 us
  Pallas kernels  31.8 us (85%)
  local copies, waits for them, and re-layouts  4.48 us (12%)
  between operations  0.66 us (2%)
    pallas_call x1, Pallas kernels, local(): pl.pallas_call(exchange, out_shape=(jax.ShapeDtypeStruct((512, LANES), F3...  30 us
    unnamed x12, local copies, waits for them, and re-layouts  4.48 us
    pallas_call x1, Pallas kernels, local(): pl.pallas_call(regroup, out_shape=(jax.ShapeDtypeStruct((chans, block), F...  1.81 us

profile of v2, /device:TPU:1, one launch (start us, length us, event | category | flops | bytes accessed | tf_op | source)
XLA Modules:
  0.0 36.9 jit_solution(7267211403715198070)
XLA Ops:
  0.6 0.0 copy-start.1
  0.6 0.9 %copy-done.1 = bf16[64,1024]{1,0:T(8,128)(2,1)S(1)} copy-done((bf16[64,1024]{1,0:T(8,128)(2,1)S(1)}, bf16[64,1024]{1,0:T(8,128)(2,1)}, u32[]{:S(2)}) %copy-start.1) | copy-done | bytes 131096
  1.5 0.0 copy-start.2
  1.5 0.9 %copy-done.2 = bf16[64,1024]{1,0:T(8,128)(2,1)S(1)} copy-done((bf16[64,1024]{1,0:T(8,128)(2,1)S(1)}, bf16[64,1024]{1,0:T(8,128)(2,1)}, u32[]{:S(2)}) %copy-start.2) | copy-done | bytes 131096
  2.4 0.0 copy-start.4
  2.4 0.7 %copy-done.4 = f32[64,16]{0,1:T(8,128)S(1)} copy-done((f32[64,16]{0,1:T(8,128)S(1)}, f32[64,16]{0,1:T(8,128)}, u32[]{:S(2)}) %copy-start.4) | copy-done | bytes 4120
  3.1 0.0 copy-start.5
  3.1 0.7 %copy-done.5 = f32[64,16]{0,1:T(8,128)S(1)} copy-done((f32[64,16]{0,1:T(8,128)S(1)}, f32[64,16]{0,1:T(8,128)}, u32[]{:S(2)}) %copy-start.5) | copy-done | bytes 4120
  3.8 30.0 %shard_map.67 = (f32[512,128]{1,0:T(8,128)S(1)}, f32[32,1,128]{2,1,0:T(1,128)S(1)}) custom-call(bf16[64,1024]{1,0:T(8,128)(2,1)S(1)} %copy-done.1, bf16[64,1024]{1,0:T(8,128)(2,1)S(1)} %copy-done.2, f32[16,64]{1,0:T(8,128)S(1)} %bitcast.4, f32[16,64]{1,0:T(8,128)S(1)} %bitcast.5), custom_call_target="tpu_custom_call" | custom-call | tf_op jit(solution)/shard_map/pallas_call | solution.py:266
  33.8 0.0 copy-start
  33.8 0.7 %copy-done = f32[512,128]{1,0:T(8,128)} copy-done((f32[512,128]{1,0:T(8,128)}, f32[512,128]{1,0:T(8,128)S(1)}, u32[]{:S(2)}) %copy-start) | copy-done | bytes 262168
  34.5 0.0 copy-start.3
  34.5 0.6 %copy-done.3 = f32[32,1,128]{2,1,0:T(1,128)} copy-done((f32[32,1,128]{2,1,0:T(1,128)}, f32[32,1,128]{2,1,0:T(1,128)S(1)}, u32[]{:S(2)}) %copy-start.3) | copy-done | bytes 16408
  35.1 1.8 %shard_map.68 = (f32[64,1024]{1,0:T(8,128)}, f32[16,64]{1,0:T(8,128)}, f32[16,64]{1,0:T(8,128)}) custom-call(f32[512,128]{1,0:T(8,128)} %copy-done, f32[32,1,128]{2,1,0:T(1,128)} %copy-done.3), custom_call_target="tpu_custom_call" | custom-call | tf_op jit(solution)/shard_map/pallas_call | solution.py:303
Async XLA Ops:
  0.6 0.9 %copy-start.1 = (bf16[64,1024]{1,0:T(8,128)(2,1)S(1)}, bf16[64,1024]{1,0:T(8,128)(2,1)}, u32[]{:S(2)}) copy-start(bf16[64,1024]{1,0:T(8,128)(2,1)} %x_hbm.1) | copy-start | bytes 393220
  1.5 0.9 %copy-start.2 = (bf16[64,1024]{1,0:T(8,128)(2,1)S(1)}, bf16[64,1024]{1,0:T(8,128)(2,1)}, u32[]{:S(2)}) copy-start(bf16[64,1024]{1,0:T(8,128)(2,1)} %g_hbm.1) | copy-start | bytes 393220
  2.4 0.7 %copy-start.4 = (f32[64,16]{0,1:T(8,128)S(1)}, f32[64,16]{0,1:T(8,128)}, u32[]{:S(2)}) copy-start(f32[64,16]{0,1:T(8,128)} %param.6) | copy-start | bytes 12292
  3.1 0.7 %copy-start.5 = (f32[64,16]{0,1:T(8,128)S(1)}, f32[64,16]{0,1:T(8,128)}, u32[]{:S(2)}) copy-start(f32[64,16]{0,1:T(8,128)} %param.7) | copy-start | bytes 12292
  33.8 0.7 %copy-start = (f32[512,128]{1,0:T(8,128)}, f32[512,128]{1,0:T(8,128)S(1)}, u32[]{:S(2)}) copy-start(f32[512,128]{1,0:T(8,128)S(1)} %get-tuple-element.8.c_ref) | copy-start | bytes 786436
  34.5 0.6 %copy-start.3 = (f32[32,1,128]{2,1,0:T(1,128)}, f32[32,1,128]{2,1,0:T(1,128)S(1)}, u32[]{:S(2)}) copy-start(f32[32,1,128]{2,1,0:T(1,128)S(1)} %get-tuple-element.9.m_ref) | copy-start | bytes 49156

commit v3 on v2

--- a/solution.py
+++ b/solution.py
@@ -35,19 +35,20 @@
     return pl.ds(pl.multiple_of(index * size, size), size)
 
 
-def to_rows(block_ref, which, stage):
+def to_rows(block_ref, stage, send):
     for ch in range(2):
         for k in range(8):
-            stage[pl.ds(16 * which + 8 * ch + k, PEERS, stride=32), :] = block_ref[
+            stage[pl.ds(8 * ch + k, PEERS, stride=16), :] = block_ref[
                 PEERS * ch : PEERS * (ch + 1), k * LANES : (k + 1) * LANES
             ].astype(F32)
+    send[...] = stage[...].astype(BF16)
 
 
 def build_toeplitz(j, recv, toep, tails):
     row = lax.broadcasted_iota(jnp.int32, (SHIFTS, LANES), 0)
     lane = lax.broadcasted_iota(jnp.int32, (SHIFTS, LANES), 1)
     keep = lane >= row
-    block = recv[pl.ds(pl.multiple_of(32 * j, 32), 16), :].astype(F32)
+    block = recv[aligned(j, 16), :].astype(F32)
     for ch in range(2):
         before = jnp.zeros((SHIFTS, LANES), F32)
         for q in range(8):
@@ -111,8 +112,8 @@
 
 def exchange(
     x_hbm, g_hbm, res_hbm, dec_hbm, recv_c, recv_m,
-    x_ref, g_ref, res_ref, dec_ref, stage, send, recv, grad, toep, tails, shifted, acc,
-    send_c, fine, coarse, send_m,
+    x_ref, g_ref, res_ref, dec_ref, stage, send_x, send_g, recv_x, recv_g, grad, toep, tails,
+    shifted, acc, send_c, fine, coarse, send_m,
     lsem, ssem_in, rsem_in, ssem_c, rsem_c, ssem_m, rsem_m,
 ):
     me = lax.axis_index("wide")
@@ -132,25 +133,27 @@
     ]
     for fetch in fetches:
         fetch.start()
-    for which, ref in ((0, x_ref), (1, g_ref)):
+    sends, recvs = (send_x, send_g), (recv_x, recv_g)
+    for which, ref in enumerate((x_ref, g_ref)):
         fetches[which].wait()
-        to_rows(ref, which, stage)
-    send[...] = stage[...].astype(BF16)
+        to_rows(ref, stage, sends[which])
     pl.semaphore_wait(barrier, PEERS - 1)
 
-    def signals_to(to, source):
+    def signals_to(which, to, source):
         return pltpu.make_async_remote_copy(
-            src_ref=send.at[aligned(to, 32), :],
-            dst_ref=recv.at[aligned(source, 32), :],
-            send_sem=ssem_in.at[to],
-            recv_sem=rsem_in.at[source],
+            src_ref=sends[which].at[aligned(to, 16), :],
+            dst_ref=recvs[which].at[aligned(source, 16), :],
+            send_sem=ssem_in.at[which, to],
+            recv_sem=rsem_in.at[which, source],
             device_id={"wide": to},
             device_id_type=MESH,
         )
 
-    for peer in peers:
-        signals_to(peer, me).start()
-    recv[aligned(me, 32), :] = send[aligned(me, 32), :]
+    for which in range(2):
+        for peer in peers:
+            signals_to(which, peer, me).start()
+    for which in range(2):
+        recvs[which][aligned(me, 16), :] = sends[which][aligned(me, 16), :]
 
     fetches[2].wait()
     fetches[3].wait()
@@ -158,34 +161,52 @@
     block_at = (lax.broadcasted_iota(jnp.int32, (256, LANES), 0) * LANES).astype(F32)
     lane_small = lax.broadcasted_iota(jnp.int32, (LANES, LANES), 1)
     offset_at = lax.broadcasted_iota(jnp.int32, (LANES, LANES), 0).astype(F32)
-    rates = []
+    factors = []
     for ch in range(2):
         rate = channel_row(dec_ref, PEERS * ch + me)
-        rates.append(rate)
-        power = jnp.exp(-rate * offset_at)
-        weighted = jnp.logical_and(lane_small >= 16, lane_small < 32)
-        fine[ch] = jnp.where(lane_small < 48, jnp.where(weighted, offset_at * power, power), 0.0)
+        factors.append(-scale * rate * channel_row(res_ref, PEERS * ch + me))
+        own = jnp.logical_and(lane_small >= 64 * ch, lane_small < 64 * ch + 48)
+        power = jnp.where(own, jnp.exp(-rate * offset_at), 0.0)
+        weighted = jnp.logical_and(lane_small % 64 >= 16, lane_small % 64 < 32)
+        power = jnp.where(weighted, offset_at * power, power)
+        upper = power.astype(BF16)
+        fine[ch, 0] = upper
+        fine[ch, 1] = upper
+        fine[ch, 2] = (power - upper.astype(F32)).astype(BF16)
         power = jnp.exp(-rate * block_at)
-        coarse[ch] = jnp.where(lane_big < 32, power, block_at * power)
-
-    build_toeplitz(me, recv, toep, tails)
-
-    def arrival(n, carry):
-        dy, dz = (n // 2) % 4, n // 8
-        dy = dy + (dy // 2) * (1 - 2 * (dy % 2))
-        dz = dz + (dz // 2) * (1 - 2 * (dz % 2))
-        source = shifted_peer(at, dz, dy, n % 2)
-        signals_to(source, source).wait_recv()
-        build_toeplitz(source, recv, toep, tails)
-        return carry
-
-    lax.fori_loop(1, PEERS, arrival, 0)
+        power = jnp.where(lane_big % 64 < 32, power, block_at * power)
+        coarse[:, 64 * ch : 64 * ch + 64] = power[:, 64 * ch : 64 * ch + 64]
+
+    def arrivals(step, first):
+        sources = []
+        for n in range(4):
+            dy, dz = 2 * (step % 2) + n // 2, step // 2
+            dy = dy + (dy // 2) * (1 - 2 * (dy % 2))
+            dz = dz + (dz // 2) * (1 - 2 * (dz % 2))
+            sources.append(shifted_peer(at, dz, dy, n % 2))
+        for n, source in enumerate(sources):
+            if n or not first:
+                signals_to(0, source, source).wait_recv()
+        for source in sources:
+            build_toeplitz(source, recv_x, toep, tails)
+
+    arrivals(0, True)
+
+    @pl.loop(1, PEERS // 4)
+    def _(step):
+        arrivals(step, False)
 
     for ch in range(2):
         toep[ch, 1:, 0:SHIFTS, :] = toep[ch, 1:, 0:SHIFTS, :] + tails[ch, : PEERS - 1]
-        grad[ch, 0:256] = (
-            recv[...].reshape(PEERS, 32, LANES)[:, 16:32].astype(F32)[:, 8 * ch : 8 * ch + 8]
-        ).reshape(256, LANES)
+
+    @pl.loop(1, PEERS)
+    def _(k):
+        peer = (me + k) % PEERS
+        signals_to(1, peer, peer).wait_recv()
+
+    for ch in range(2):
+        rows = recv_g[...].reshape(PEERS, 16, LANES).astype(F32)[:, 8 * ch : 8 * ch + 8]
+        grad[ch, 0:256] = rows.reshape(256, LANES)
         grad[ch, 256:] = jnp.zeros((16, LANES), F32)
         build_shifted(ch, grad, shifted)
 
@@ -199,25 +220,27 @@
             device_id_type=MESH,
         )
 
-    def modal(ch):
-        part = jnp.dot(
-            send_c[ch], fine[ch], precision=lax.Precision.HIGHEST, preferred_element_type=F32
-        )
-        sums = jnp.sum(part * coarse[ch], axis=0, keepdims=True)
-        both = sums + pltpu.roll(sums, LANES - 16, 1)
-        residue = channel_row(res_ref, PEERS * ch + me)
-        lane = lax.broadcasted_iota(jnp.int32, (1, LANES), 1)
-        line = jnp.where(lane < 16, scale * sums, -scale * rates[ch] * residue * both)
-        return jnp.where(lane < 32, line, 0.0)
-
-    lines = []
     for ch in range(2):
         send_c[ch] = correlate(ch, toep, shifted, acc, scale)
         for peer in peers:
             lags_to(ch, peer, me).start()
         recv_c[pl.ds(pl.multiple_of(16 * me + 8 * ch, 8), 8), :] = send_c[ch, aligned(me, 8), :]
-        lines.append(modal(ch))
-    line = lines[0] + pltpu.roll(lines[1], 32, 1)
+
+    parts = []
+    for ch in range(2):
+        lags = send_c[ch]
+        upper = lags.astype(BF16)
+        parts += [upper, (lags - upper.astype(F32)).astype(BF16), upper]
+    mixed = jnp.dot(
+        jnp.concatenate(parts, axis=1),
+        fine[...].reshape(6 * LANES, LANES),
+        preferred_element_type=F32,
+    )
+    sums = jnp.sum(mixed * coarse[...], axis=0, keepdims=True)
+    both = sums + pltpu.roll(sums, LANES - 16, 1)
+    lane = lax.broadcasted_iota(jnp.int32, (1, LANES), 1)
+    factor = jnp.where(lane < 64, factors[0], factors[1])
+    line = jnp.where(lane % 64 < 16, scale * sums, factor * both)
     send_m[...] = line
     recv_m[me] = line
 
@@ -237,7 +260,8 @@
     @pl.loop(1, PEERS)
     def _(k):
         peer = (me + k) % PEERS
-        signals_to(peer, me).wait_send()
+        signals_to(0, peer, me).wait_send()
+        signals_to(1, peer, me).wait_send()
         lags_to(0, peer, me).wait_send()
         lags_to(1, peer, me).wait_send()
         modes_to(peer, me).wait_send()
@@ -253,8 +277,8 @@
                 pl.ds(8 * ch + k, PEERS, stride=16), :
             ]
     lines = jnp.transpose(m_ref[:, 0, :])
-    rg_ref[...] = jnp.concatenate([lines[0:16], lines[32:48]], axis=1)
-    ld_ref[...] = jnp.concatenate([lines[16:32], lines[48:64]], axis=1)
+    rg_ref[...] = jnp.concatenate([lines[0:16], lines[64:80]], axis=1)
+    ld_ref[...] = jnp.concatenate([lines[16:32], lines[80:96]], axis=1)
 
 
 def local(inputs, out_grad, residues, decay):
@@ -276,21 +300,23 @@
             pltpu.VMEM((chans, block), BF16),
             pltpu.VMEM((modes, chans), F32),
             pltpu.VMEM((modes, chans), F32),
-            pltpu.VMEM((1024, LANES), F32),
-            pltpu.VMEM((1024, LANES), BF16),
-            pltpu.VMEM((1024, LANES), BF16),
+            pltpu.VMEM((512, LANES), F32),
+            pltpu.VMEM((512, LANES), BF16),
+            pltpu.VMEM((512, LANES), BF16),
+            pltpu.VMEM((512, LANES), BF16),
+            pltpu.VMEM((512, LANES), BF16),
             pltpu.VMEM((2, 272, LANES), F32),
             pltpu.VMEM((2, PEERS, 256, LANES), BF16),
             pltpu.VMEM((2, PEERS, SHIFTS, LANES), BF16),
             pltpu.VMEM((2, 1024, 256), BF16),
             pltpu.VMEM((TURNS, 2, 264, LANES), F32),
             pltpu.VMEM((2, 256, LANES), F32),
-            pltpu.VMEM((2, LANES, LANES), F32),
-            pltpu.VMEM((2, 256, LANES), F32),
+            pltpu.VMEM((2, 3, LANES, LANES), BF16),
+            pltpu.VMEM((256, LANES), F32),
             pltpu.VMEM((1, LANES), F32),
             dma((4,)),
-            dma((PEERS,)),
-            dma((PEERS,)),
+            dma((2, PEERS)),
+            dma((2, PEERS)),
             dma((2, PEERS)),
             dma((2, PEERS)),
             dma((PEERS,)),
@@ -299,7 +325,7 @@
         compiler_params=pltpu.CompilerParams(
             collective_id=0, has_side_effects=True, vmem_limit_bytes=32 * 2**20
         ),
-    )(inputs, out_grad, residues.T, decay.T)
+    )(*(pltpu.with_memory_space_constraint(a, pltpu.HBM) for a in (inputs, out_grad, residues.T, decay.T)))
     filter_grad, residue_grad, log_decay_grad = pl.pallas_call(
         regroup,
         out_shape=(
@@ -309,6 +335,7 @@
         ),
         in_specs=[vmem] * 2,
         out_specs=(vmem,) * 3,
+        compiler_params=pltpu.CompilerParams(vmem_limit_bytes=4 * 2**20),
     )(lags, lines)
     return filter_grad, residue_grad.T, log_decay_grad.T
 

time: 37.2 us -> 30.1 us (0.81)
  local copies, waits for them, and re-layouts: 4.48 us -> 0 us
  Pallas kernels: 31.8 us -> 29.3 us
    unnamed x12 -> x0, local copies, waits for them, and re-layouts: 4.48 us -> none
    pallas_call x1, Pallas kernels: 30 us -> 28.4 us  [local(): pl.pallas_call(exchange, out_shape=(jax.ShapeDtypeStruct((512, LANES), F3...]
    pallas_call x1, Pallas kernels: 1.81 us -> 0.87 us  [local(): pl.pallas_call(regroup, out_shape=(jax.ShapeDtypeStruct((chans, block), F...]
where the time goes in v3:
time: 30.1 us; the launch traced here: 29.9 us
  Pallas kernels  29.3 us (97%)
  between operations  0.64 us (2%)
    pallas_call x1, Pallas kernels, local(): pl.pallas_call(exchange, out_shape=(jax.ShapeDtypeStruct((512, LANES), F3...  28.4 us
    pallas_call x1, Pallas kernels, local(): pl.pallas_call(regroup, out_shape=(jax.ShapeDtypeStruct((chans, block), F...  0.87 us

profile of v3, /device:TPU:1, one launch (start us, length us, event | category | flops | bytes accessed | tf_op | source)
XLA Modules:
  0.0 29.9 jit_solution(5278830918571509434)
XLA Ops:
  0.6 28.4 %shard_map.67 = (f32[512,128]{1,0:T(8,128)S(1)}, f32[32,1,128]{2,1,0:T(1,128)S(1)}) custom-call(bf16[64,1024]{1,0:T(8,128)(2,1)} %x_hbm.1, bf16[64,1024]{1,0:T(8,128)(2,1)} %g_hbm.1, f32[16,64]{1,0:T(8,128)} %bitcast.4, f32[16,64]{1,0:T(8,128)} %bitcast.5), custom_call_target="tpu_custom_call" | custom-call | tf_op jit(solution)/shard_map/pallas_call | solution.py:290
  29.1 0.9 %shard_map.68 = (f32[64,1024]{1,0:T(8,128)}, f32[16,64]{1,0:T(8,128)}, f32[16,64]{1,0:T(8,128)}) custom-call(f32[512,128]{1,0:T(8,128)S(1)} %get-tuple-element.8.c_ref, f32[32,1,128]{2,1,0:T(1,128)S(1)} %get-tuple-element.9.m_ref), custom_call_target="tpu_custom_call" | custom-call | tf_op jit(solution)/shard_map/pallas_call | solution.py:329

commit v4 on v3

--- a/solution.py
+++ b/solution.py
@@ -16,6 +16,7 @@
 TURNS = LANES // SHIFTS
 PEERS = 32
 RING = (0, 1, 2, 1)
+NEAR = (0, 1, 3, 2)
 OFFSETS = sorted(
     ((dz, dy, dc) for dz in range(4) for dy in range(4) for dc in range(2) if dz or dy or dc),
     key=lambda o: (-RING[o[0]] - RING[o[1]], -o[2], o),
@@ -31,24 +32,32 @@
     return ((z + dz) % 4) * 8 + ((y + dy) % 4) * 2 + (core + dc) % 2
 
 
+def group_of(dz, dy, dc):
+    return 2 * NEAR.index(dz) + NEAR.index(dy) // 2
+
+
 def aligned(index, size):
     return pl.ds(pl.multiple_of(index * size, size), size)
 
 
-def to_rows(block_ref, stage, send):
+def to_rows(block_ref, which, stage):
     for ch in range(2):
         for k in range(8):
-            stage[pl.ds(8 * ch + k, PEERS, stride=16), :] = block_ref[
+            stage[pl.ds(16 * which + 8 * ch + k, PEERS, stride=32), :] = block_ref[
                 PEERS * ch : PEERS * (ch + 1), k * LANES : (k + 1) * LANES
             ].astype(F32)
-    send[...] = stage[...].astype(BF16)
+
+
+def wait_rows(ref, rows, sem):
+    part = ref.at[0:rows]
+    pltpu.make_async_copy(part, part, sem).wait()
 
 
 def build_toeplitz(j, recv, toep, tails):
     row = lax.broadcasted_iota(jnp.int32, (SHIFTS, LANES), 0)
     lane = lax.broadcasted_iota(jnp.int32, (SHIFTS, LANES), 1)
     keep = lane >= row
-    block = recv[aligned(j, 16), :].astype(F32)
+    block = recv[pl.ds(pl.multiple_of(32 * j, 32), 16), :].astype(F32)
     for ch in range(2):
         before = jnp.zeros((SHIFTS, LANES), F32)
         for q in range(8):
@@ -112,9 +121,9 @@
 
 def exchange(
     x_hbm, g_hbm, res_hbm, dec_hbm, recv_c, recv_m,
-    x_ref, g_ref, res_ref, dec_ref, stage, send_x, send_g, recv_x, recv_g, grad, toep, tails,
-    shifted, acc, send_c, fine, coarse, send_m,
-    lsem, ssem_in, rsem_in, ssem_c, rsem_c, ssem_m, rsem_m,
+    x_ref, g_ref, res_ref, dec_ref, stage, send, recv, grad, toep, tails, shifted,
+    acc, send_c, fine, coarse, send_m,
+    fetched, sent_in, come_in, sent_c, come_c, sent_m, come_m,
 ):
     me = lax.axis_index("wide")
     at = place(me)
@@ -126,34 +135,30 @@
         pl.semaphore_signal(barrier, inc=1, device_id={"wide": peer}, device_id_type=MESH)
 
     fetches = [
-        pltpu.make_async_copy(src, dst, lsem.at[n])
+        pltpu.make_async_copy(src, dst, fetched.at[n])
         for n, (src, dst) in enumerate(
             ((x_hbm, x_ref), (g_hbm, g_ref), (dec_hbm, dec_ref), (res_hbm, res_ref))
         )
     ]
     for fetch in fetches:
         fetch.start()
-    sends, recvs = (send_x, send_g), (recv_x, recv_g)
     for which, ref in enumerate((x_ref, g_ref)):
         fetches[which].wait()
-        to_rows(ref, stage, sends[which])
+        to_rows(ref, which, stage)
+    send[...] = stage[...].astype(BF16)
     pl.semaphore_wait(barrier, PEERS - 1)
 
-    def signals_to(which, to, source):
-        return pltpu.make_async_remote_copy(
-            src_ref=sends[which].at[aligned(to, 16), :],
-            dst_ref=recvs[which].at[aligned(source, 16), :],
-            send_sem=ssem_in.at[which, to],
-            recv_sem=rsem_in.at[which, source],
-            device_id={"wide": to},
+    for peer, offset in zip(peers, OFFSETS):
+        back = tuple(-d % n for d, n in zip(offset, (4, 4, 2)))
+        pltpu.make_async_remote_copy(
+            src_ref=send.at[aligned(peer, 32), :],
+            dst_ref=recv.at[aligned(me, 32), :],
+            send_sem=sent_in,
+            recv_sem=come_in.at[group_of(*back)],
+            device_id={"wide": peer},
             device_id_type=MESH,
-        )
-
-    for which in range(2):
-        for peer in peers:
-            signals_to(which, peer, me).start()
-    for which in range(2):
-        recvs[which][aligned(me, 16), :] = sends[which][aligned(me, 16), :]
+        ).start()
+    recv[aligned(me, 32), :] = send[aligned(me, 32), :]
 
     fetches[2].wait()
     fetches[3].wait()
@@ -177,58 +182,46 @@
         power = jnp.where(lane_big % 64 < 32, power, block_at * power)
         coarse[:, 64 * ch : 64 * ch + 64] = power[:, 64 * ch : 64 * ch + 64]
 
-    def arrivals(step, first):
-        sources = []
+    def arrivals(group, senders):
+        wait_rows(recv, 32 * senders, come_in.at[group])
         for n in range(4):
-            dy, dz = 2 * (step % 2) + n // 2, step // 2
+            dy, dz = 2 * (group % 2) + n // 2, group // 2
             dy = dy + (dy // 2) * (1 - 2 * (dy % 2))
             dz = dz + (dz // 2) * (1 - 2 * (dz % 2))
-            sources.append(shifted_peer(at, dz, dy, n % 2))
-        for n, source in enumerate(sources):
-            if n or not first:
-                signals_to(0, source, source).wait_recv()
-        for source in sources:
-            build_toeplitz(source, recv_x, toep, tails)
-
-    arrivals(0, True)
-
-    @pl.loop(1, PEERS // 4)
-    def _(step):
-        arrivals(step, False)
+            build_toeplitz(shifted_peer(at, dz, dy, n % 2), recv, toep, tails)
+
+    arrivals(0, 3)
+
+    @pl.loop(1, 8)
+    def _(group):
+        arrivals(group, 4)
 
     for ch in range(2):
         toep[ch, 1:, 0:SHIFTS, :] = toep[ch, 1:, 0:SHIFTS, :] + tails[ch, : PEERS - 1]
 
-    @pl.loop(1, PEERS)
-    def _(k):
-        peer = (me + k) % PEERS
-        signals_to(1, peer, peer).wait_recv()
-
-    for ch in range(2):
-        rows = recv_g[...].reshape(PEERS, 16, LANES).astype(F32)[:, 8 * ch : 8 * ch + 8]
+    for ch in range(2):
+        rows = recv[...].reshape(PEERS, 32, LANES)[:, 16:32].astype(F32)[:, 8 * ch : 8 * ch + 8]
         grad[ch, 0:256] = rows.reshape(256, LANES)
         grad[ch, 256:] = jnp.zeros((16, LANES), F32)
         build_shifted(ch, grad, shifted)
 
-    def lags_to(ch, to, source):
-        return pltpu.make_async_remote_copy(
-            src_ref=send_c.at[ch, aligned(to, 8), :],
-            dst_ref=recv_c.at[pl.ds(pl.multiple_of(16 * source + 8 * ch, 8), 8), :],
-            send_sem=ssem_c.at[ch, to],
-            recv_sem=rsem_c.at[ch, source],
-            device_id={"wide": to},
+    for ch in range(2):
+        lags = correlate(ch, toep, shifted, acc, scale)
+        send_c[:, 8 * ch : 8 * ch + 8, :] = lags.reshape(PEERS, 8, LANES)
+    for peer in peers:
+        pltpu.make_async_remote_copy(
+            src_ref=send_c.at[peer],
+            dst_ref=recv_c.at[me],
+            send_sem=sent_c,
+            recv_sem=come_c,
+            device_id={"wide": peer},
             device_id_type=MESH,
-        )
-
-    for ch in range(2):
-        send_c[ch] = correlate(ch, toep, shifted, acc, scale)
-        for peer in peers:
-            lags_to(ch, peer, me).start()
-        recv_c[pl.ds(pl.multiple_of(16 * me + 8 * ch, 8), 8), :] = send_c[ch, aligned(me, 8), :]
+        ).start()
+    recv_c[me] = send_c[me]
 
     parts = []
     for ch in range(2):
-        lags = send_c[ch]
+        lags = send_c[:, 8 * ch : 8 * ch + 8, :].reshape(256, LANES)
         upper = lags.astype(BF16)
         parts += [upper, (lags - upper.astype(F32)).astype(BF16), upper]
     mixed = jnp.dot(
@@ -244,37 +237,28 @@
     send_m[...] = line
     recv_m[me] = line
 
-    def modes_to(to, source):
-        return pltpu.make_async_remote_copy(
+    for peer in peers:
+        pltpu.make_async_remote_copy(
             src_ref=send_m,
-            dst_ref=recv_m.at[source],
-            send_sem=ssem_m.at[to],
-            recv_sem=rsem_m.at[source],
-            device_id={"wide": to},
+            dst_ref=recv_m.at[me],
+            send_sem=sent_m,
+            recv_sem=come_m,
+            device_id={"wide": peer},
             device_id_type=MESH,
-        )
-
-    for peer in peers:
-        modes_to(peer, me).start()
-
-    @pl.loop(1, PEERS)
-    def _(k):
-        peer = (me + k) % PEERS
-        signals_to(0, peer, me).wait_send()
-        signals_to(1, peer, me).wait_send()
-        lags_to(0, peer, me).wait_send()
-        lags_to(1, peer, me).wait_send()
-        modes_to(peer, me).wait_send()
-        lags_to(0, peer, peer).wait_recv()
-        lags_to(1, peer, peer).wait_recv()
-        modes_to(peer, peer).wait_recv()
+        ).start()
+
+    wait_rows(send, 32 * (PEERS - 1), sent_in)
+    wait_rows(send_c, PEERS - 1, sent_c)
+    wait_rows(recv_m, PEERS - 1, sent_m)
+    wait_rows(recv_c, PEERS - 1, come_c)
+    wait_rows(recv_m, PEERS - 1, come_m)
 
 
 def regroup(c_ref, m_ref, out_ref, rg_ref, ld_ref):
     for ch in range(2):
         for k in range(8):
             out_ref[PEERS * ch : PEERS * (ch + 1), k * LANES : (k + 1) * LANES] = c_ref[
-                pl.ds(8 * ch + k, PEERS, stride=16), :
+                :, 8 * ch + k, :
             ]
     lines = jnp.transpose(m_ref[:, 0, :])
     rg_ref[...] = jnp.concatenate([lines[0:16], lines[64:80]], axis=1)
@@ -290,7 +274,7 @@
     lags, lines = pl.pallas_call(
         exchange,
         out_shape=(
-            jax.ShapeDtypeStruct((512, LANES), F32),
+            jax.ShapeDtypeStruct((PEERS, 16, LANES), F32),
             jax.ShapeDtypeStruct((PEERS, 1, LANES), F32),
         ),
         in_specs=[hbm] * 4,
@@ -300,27 +284,25 @@
             pltpu.VMEM((chans, block), BF16),
             pltpu.VMEM((modes, chans), F32),
             pltpu.VMEM((modes, chans), F32),
-            pltpu.VMEM((512, LANES), F32),
-            pltpu.VMEM((512, LANES), BF16),
-            pltpu.VMEM((512, LANES), BF16),
-            pltpu.VMEM((512, LANES), BF16),
-            pltpu.VMEM((512, LANES), BF16),
+            pltpu.VMEM((1024, LANES), F32),
+            pltpu.VMEM((1024, LANES), BF16),
+            pltpu.VMEM((1024, LANES), BF16),
             pltpu.VMEM((2, 272, LANES), F32),
             pltpu.VMEM((2, PEERS, 256, LANES), BF16),
             pltpu.VMEM((2, PEERS, SHIFTS, LANES), BF16),
             pltpu.VMEM((2, 1024, 256), BF16),
             pltpu.VMEM((TURNS, 2, 264, LANES), F32),
-            pltpu.VMEM((2, 256, LANES), F32),
+            pltpu.VMEM((PEERS, 16, LANES), F32),
             pltpu.VMEM((2, 3, LANES, LANES), BF16),
             pltpu.VMEM((256, LANES), F32),
             pltpu.VMEM((1, LANES), F32),
             dma((4,)),
-            dma((2, PEERS)),
-            dma((2, PEERS)),
-            dma((2, PEERS)),
-            dma((2, PEERS)),
-            dma((PEERS,)),
-            dma((PEERS,)),
+            dma,
+            dma((8,)),
+            dma,
+            dma,
+            dma,
+            dma,
         ],
         compiler_params=pltpu.CompilerParams(
             collective_id=0, has_side_effects=True, vmem_limit_bytes=32 * 2**20

time: 30.1 us -> 25.7 us (0.85)
  Pallas kernels: 29.3 us -> 24.9 us
    pallas_call x1, Pallas kernels: 28.4 us -> 24 us  [local(): pl.pallas_call(exchange, out_shape=(jax.ShapeDtypeStruct((PEERS, 16, LANE...]
where the time goes in v4:
time: 25.7 us; the launch traced here: 25.6 us
  Pallas kernels  24.9 us (97%)
  between operations  0.64 us (2%)
    pallas_call x1, Pallas kernels, local(): pl.pallas_call(exchange, out_shape=(jax.ShapeDtypeStruct((PEERS, 16, LANE...  24 us
    pallas_call x1, Pallas kernels, local(): pl.pallas_call(regroup, out_shape=(jax.ShapeDtypeStruct((chans, block), F...  0.94 us

profile of v4, /device:TPU:1, one launch (start us, length us, event | category | flops | bytes accessed | tf_op | source)
XLA Modules:
  0.0 25.6 jit_solution(10887381062273558804)
XLA Ops:
  0.6 24.0 %shard_map.67 = (f32[32,16,128]{2,1,0:T(8,128)S(1)}, f32[32,1,128]{2,1,0:T(1,128)S(1)}) custom-call(bf16[64,1024]{1,0:T(8,128)(2,1)} %x_hbm.1, bf16[64,1024]{1,0:T(8,128)(2,1)} %g_hbm.1, f32[16,64]{1,0:T(8,128)} %bitcast.4, f32[16,64]{1,0:T(8,128)} %bitcast.5), custom_call_target="tpu_custom_call" | custom-call | tf_op jit(solution)/shard_map/pallas_call | solution.py:274
  24.6 0.9 %shard_map.68 = (f32[64,1024]{1,0:T(8,128)}, f32[16,64]{1,0:T(8,128)}, f32[16,64]{1,0:T(8,128)}) custom-call(f32[32,16,128]{2,1,0:T(8,128)S(1)} %get-tuple-element.8.c_ref, f32[32,1,128]{2,1,0:T(1,128)S(1)} %get-tuple-element.9.m_ref), custom_call_target="tpu_custom_call" | custom-call | tf_op jit(solution)/shard_map/pallas_call | solution.py:311

commit v5 on v4

--- a/solution.py
+++ b/solution.py
@@ -16,7 +16,6 @@
 TURNS = LANES // SHIFTS
 PEERS = 32
 RING = (0, 1, 2, 1)
-NEAR = (0, 1, 3, 2)
 OFFSETS = sorted(
     ((dz, dy, dc) for dz in range(4) for dy in range(4) for dc in range(2) if dz or dy or dc),
     key=lambda o: (-RING[o[0]] - RING[o[1]], -o[2], o),
@@ -32,10 +31,6 @@
     return ((z + dz) % 4) * 8 + ((y + dy) % 4) * 2 + (core + dc) % 2
 
 
-def group_of(dz, dy, dc):
-    return 2 * NEAR.index(dz) + NEAR.index(dy) // 2
-
-
 def aligned(index, size):
     return pl.ds(pl.multiple_of(index * size, size), size)
 
@@ -53,19 +48,19 @@
     pltpu.make_async_copy(part, part, sem).wait()
 
 
-def build_toeplitz(j, recv, toep, tails):
+def toeplitz(ch, i, signal, before):
     row = lax.broadcasted_iota(jnp.int32, (SHIFTS, LANES), 0)
     lane = lax.broadcasted_iota(jnp.int32, (SHIFTS, LANES), 1)
-    keep = lane >= row
-    block = recv[pl.ds(pl.multiple_of(32 * j, 32), 16), :].astype(F32)
-    for ch in range(2):
-        before = jnp.zeros((SHIFTS, LANES), F32)
+    halves = []
+    for p in range(2):
+        rows = []
         for q in range(8):
-            spread = jnp.broadcast_to(block[8 * ch + q : 8 * ch + q + 1], (SHIFTS, LANES))
+            spread = jnp.broadcast_to(signal[ch, pl.ds(16 * i + 8 * p + q, 1), :], (SHIFTS, LANES))
             now = pltpu.roll(spread, 0, 1, stride=1, stride_axis=0)
-            toep[ch, j, q * SHIFTS : (q + 1) * SHIFTS, :] = jnp.where(keep, now, before).astype(BF16)
+            rows.append(jnp.where(lane >= row, now, before).astype(BF16))
             before = now
-        tails[ch, j] = jnp.where(keep, 0.0, before).astype(BF16)
+        halves.append(jnp.concatenate(rows, axis=0))
+    return jnp.concatenate(halves, axis=1), before
 
 
 def build_shifted(ch, grad, shifted):
@@ -81,11 +76,12 @@
     shifted[ch] = jnp.stack(turns, axis=1).reshape(1024, 256).astype(BF16)
 
 
-def correlate(ch, toep, shifted, acc, scale):
-    acc[...] = jnp.zeros_like(acc)
+def correlate(ch, signal, shifted, acc, scale):
+    acc[:, :, 256:, :] = jnp.zeros((TURNS, 2, 8, LANES), F32)
+    before = jnp.zeros((SHIFTS, LANES), F32)
     for i in range(16):
         live = 256 - 16 * i
-        table = jnp.concatenate([toep[ch, 2 * i], toep[ch, 2 * i + 1]], axis=1)
+        table, before = toeplitz(ch, i, signal, before)
         part = lax.dot_general(
             shifted[ch, 64 * i : 1024, :],
             table,
@@ -94,8 +90,9 @@
         ).reshape(live // 8, TURNS, 8, 256)
         for h in range(TURNS):
             own = part[:, h].reshape(live, 256)
-            acc[h, 0, 0:live] += own[:, :LANES]
-            acc[h, 1, 0:live] += own[:, LANES:]
+            for half in range(2):
+                term = own[:, half * LANES : (half + 1) * LANES]
+                acc[h, half, 0:live] = acc[h, half, 0:live] + term if i else term
     group = lax.broadcasted_iota(jnp.int32, (256, LANES), 1) // SHIFTS
     total = None
     for turn in range(TURNS):
@@ -121,7 +118,7 @@
 
 def exchange(
     x_hbm, g_hbm, res_hbm, dec_hbm, recv_c, recv_m,
-    x_ref, g_ref, res_ref, dec_ref, stage, send, recv, grad, toep, tails, shifted,
+    x_ref, g_ref, res_ref, dec_ref, stage, send, recv, signal, grad, shifted,
     acc, send_c, fine, coarse, send_m,
     fetched, sent_in, come_in, sent_c, come_c, sent_m, come_m,
 ):
@@ -148,13 +145,12 @@
     send[...] = stage[...].astype(BF16)
     pl.semaphore_wait(barrier, PEERS - 1)
 
-    for peer, offset in zip(peers, OFFSETS):
-        back = tuple(-d % n for d, n in zip(offset, (4, 4, 2)))
+    for peer in peers:
         pltpu.make_async_remote_copy(
             src_ref=send.at[aligned(peer, 32), :],
             dst_ref=recv.at[aligned(me, 32), :],
             send_sem=sent_in,
-            recv_sem=come_in.at[group_of(*back)],
+            recv_sem=come_in,
             device_id={"wide": peer},
             device_id_type=MESH,
         ).start()
@@ -182,31 +178,16 @@
         power = jnp.where(lane_big % 64 < 32, power, block_at * power)
         coarse[:, 64 * ch : 64 * ch + 64] = power[:, 64 * ch : 64 * ch + 64]
 
-    def arrivals(group, senders):
-        wait_rows(recv, 32 * senders, come_in.at[group])
-        for n in range(4):
-            dy, dz = 2 * (group % 2) + n // 2, group // 2
-            dy = dy + (dy // 2) * (1 - 2 * (dy % 2))
-            dz = dz + (dz // 2) * (1 - 2 * (dz % 2))
-            build_toeplitz(shifted_peer(at, dz, dy, n % 2), recv, toep, tails)
-
-    arrivals(0, 3)
-
-    @pl.loop(1, 8)
-    def _(group):
-        arrivals(group, 4)
-
-    for ch in range(2):
-        toep[ch, 1:, 0:SHIFTS, :] = toep[ch, 1:, 0:SHIFTS, :] + tails[ch, : PEERS - 1]
-
-    for ch in range(2):
-        rows = recv[...].reshape(PEERS, 32, LANES)[:, 16:32].astype(F32)[:, 8 * ch : 8 * ch + 8]
-        grad[ch, 0:256] = rows.reshape(256, LANES)
+    wait_rows(recv, 32 * (PEERS - 1), come_in)
+    for ch in range(2):
+        rows = recv[...].astype(F32).reshape(PEERS, 32, LANES)
+        signal[ch] = rows[:, 8 * ch : 8 * ch + 8].reshape(256, LANES)
+        grad[ch, 0:256] = rows[:, 8 * ch + 16 : 8 * ch + 24].reshape(256, LANES)
         grad[ch, 256:] = jnp.zeros((16, LANES), F32)
         build_shifted(ch, grad, shifted)
 
     for ch in range(2):
-        lags = correlate(ch, toep, shifted, acc, scale)
+        lags = correlate(ch, signal, shifted, acc, scale)
         send_c[:, 8 * ch : 8 * ch + 8, :] = lags.reshape(PEERS, 8, LANES)
     for peer in peers:
         pltpu.make_async_remote_copy(
@@ -287,9 +268,8 @@
             pltpu.VMEM((1024, LANES), F32),
             pltpu.VMEM((1024, LANES), BF16),
             pltpu.VMEM((1024, LANES), BF16),
+            pltpu.VMEM((2, 256, LANES), F32),
             pltpu.VMEM((2, 272, LANES), F32),
-            pltpu.VMEM((2, PEERS, 256, LANES), BF16),
-            pltpu.VMEM((2, PEERS, SHIFTS, LANES), BF16),
             pltpu.VMEM((2, 1024, 256), BF16),
             pltpu.VMEM((TURNS, 2, 264, LANES), F32),
             pltpu.VMEM((PEERS, 16, LANES), F32),
@@ -298,7 +278,7 @@
             pltpu.VMEM((1, LANES), F32),
             dma((4,)),
             dma,
-            dma((8,)),
+            dma,
             dma,
             dma,
             dma,

time: 25.7 us -> 24.4 us (0.949)
  Pallas kernels: 24.9 us -> 23.6 us
    pallas_call x1, Pallas kernels: 24 us -> 22.7 us  [local(): pl.pallas_call(exchange, out_shape=(jax.ShapeDtypeStruct((PEERS, 16, LANE...]
where the time goes in v5:
time: 24.4 us; the launch traced here: 24.2 us
  Pallas kernels  23.6 us (97%)
  between operations  0.64 us (3%)
    pallas_call x1, Pallas kernels, local(): pl.pallas_call(exchange, out_shape=(jax.ShapeDtypeStruct((PEERS, 16, LANE...  22.7 us
    pallas_call x1, Pallas kernels, local(): pl.pallas_call(regroup, out_shape=(jax.ShapeDtypeStruct((chans, block), F...  0.94 us

profile of v5, /device:TPU:1, one launch (start us, length us, event | category | flops | bytes accessed | tf_op | source)
XLA Modules:
  0.0 24.2 jit_solution(1841034721906791034)
XLA Ops:
  0.6 22.7 %shard_map.67 = (f32[32,16,128]{2,1,0:T(8,128)S(1)}, f32[32,1,128]{2,1,0:T(1,128)S(1)}) custom-call(bf16[64,1024]{1,0:T(8,128)(2,1)} %x_hbm.1, bf16[64,1024]{1,0:T(8,128)(2,1)} %g_hbm.1, f32[16,64]{1,0:T(8,128)} %bitcast.4, f32[16,64]{1,0:T(8,128)} %bitcast.5), custom_call_target="tpu_custom_call" | custom-call | tf_op jit(solution)/shard_map/pallas_call | solution.py:255
  23.3 0.9 %shard_map.68 = (f32[64,1024]{1,0:T(8,128)}, f32[16,64]{1,0:T(8,128)}, f32[16,64]{1,0:T(8,128)}) custom-call(f32[32,16,128]{2,1,0:T(8,128)S(1)} %get-tuple-element.8.c_ref, f32[32,1,128]{2,1,0:T(1,128)S(1)} %get-tuple-element.9.m_ref), custom_call_target="tpu_custom_call" | custom-call | tf_op jit(solution)/shard_map/pallas_call | solution.py:291

commit v6 on v5

--- a/solution.py
+++ b/solution.py
@@ -48,58 +48,68 @@
     pltpu.make_async_copy(part, part, sem).wait()
 
 
-def toeplitz(ch, i, signal, before):
+def turned(ch, m, signal):
+    if m < 0:
+        return jnp.zeros((SHIFTS, LANES), F32)
+    spread = jnp.broadcast_to(signal[ch, pl.ds(m, 1), :], (SHIFTS, LANES))
+    return pltpu.roll(spread, 0, 1, stride=1, stride_axis=0)
+
+
+def toeplitz(ch, i, signal, now):
     row = lax.broadcasted_iota(jnp.int32, (SHIFTS, LANES), 0)
     lane = lax.broadcasted_iota(jnp.int32, (SHIFTS, LANES), 1)
-    halves = []
-    for p in range(2):
-        rows = []
-        for q in range(8):
-            spread = jnp.broadcast_to(signal[ch, pl.ds(16 * i + 8 * p + q, 1), :], (SHIFTS, LANES))
-            now = pltpu.roll(spread, 0, 1, stride=1, stride_axis=0)
-            rows.append(jnp.where(lane >= row, now, before).astype(BF16))
-            before = now
-        halves.append(jnp.concatenate(rows, axis=0))
-    return jnp.concatenate(halves, axis=1), before
-
-
-def build_shifted(ch, grad, shifted):
-    lane = lax.broadcasted_iota(jnp.int32, (264, LANES), 1)
-    here = grad[ch, 0:264, :]
-    after = grad[ch, 1:265, :]
+    rows = []
+    for m in range(16 * i + 15, 16 * i - 1, -1):
+        before = turned(ch, m - 1, signal)
+        rows.insert(0, jnp.where(lane >= row, now, before).astype(BF16))
+        now = before
+    halves = [jnp.concatenate(rows[:8], axis=0), jnp.concatenate(rows[8:], axis=0)]
+    return jnp.concatenate(halves, axis=1), now
+
+
+def build_shifted(ch, plane, grad, shifted):
+    first = 64 * plane
+    lane = lax.broadcasted_iota(jnp.int32, (72, LANES), 1)
+    here = grad[ch, first : first + 72, :]
+    after = grad[ch, first + 1 : first + 73, :]
     turns = []
     for h in range(TURNS):
         moved = here
         if h:
             moved = pltpu.roll(jnp.where(lane < SHIFTS * h, after, here), LANES - SHIFTS * h, 1)
-        turns.append(jnp.concatenate([moved[0:256], moved[8:264]], axis=1).reshape(32, 8, 256))
-    shifted[ch] = jnp.stack(turns, axis=1).reshape(1024, 256).astype(BF16)
-
-
-def correlate(ch, signal, shifted, acc, scale):
-    acc[:, :, 256:, :] = jnp.zeros((TURNS, 2, 8, LANES), F32)
-    before = jnp.zeros((SHIFTS, LANES), F32)
-    for i in range(16):
-        live = 256 - 16 * i
-        table, before = toeplitz(ch, i, signal, before)
-        part = lax.dot_general(
-            shifted[ch, 64 * i : 1024, :],
-            table,
-            (((1,), (1,)), ((), ())),
-            preferred_element_type=F32,
-        ).reshape(live // 8, TURNS, 8, 256)
-        for h in range(TURNS):
-            own = part[:, h].reshape(live, 256)
-            for half in range(2):
-                term = own[:, half * LANES : (half + 1) * LANES]
-                acc[h, half, 0:live] = acc[h, half, 0:live] + term if i else term
+        turns.append(jnp.concatenate([moved[0:64], moved[8:72]], axis=1).reshape(8, 8, 256))
+    shifted[ch, 4 * first : 4 * first + 256] = (
+        jnp.stack(turns, axis=1).reshape(256, 256).astype(BF16)
+    )
+
+
+def add_chunk(ch, i, signal, shifted, acc, now):
+    live = 256 - 16 * i
+    table, now = toeplitz(ch, i, signal, now)
+    part = lax.dot_general(
+        shifted[ch, 64 * i : 1024, :],
+        table,
+        (((1,), (1,)), ((), ())),
+        preferred_element_type=F32,
+    ).reshape(live // 8, TURNS, 8, 256)
+    for h in range(TURNS):
+        own = part[:, h].reshape(live, 256)
+        for half in range(2):
+            term = own[:, half * LANES : (half + 1) * LANES]
+            if live > 16:
+                acc[ch, h, half, 0 : live - 16] = acc[ch, h, half, 0 : live - 16] + term[: live - 16]
+            acc[ch, h, half, live - 16 : live] = term[live - 16 :]
+    return now
+
+
+def regroup_lags(ch, acc, scale):
     group = lax.broadcasted_iota(jnp.int32, (256, LANES), 1) // SHIFTS
     total = None
     for turn in range(TURNS):
         mixed = None
         for low in range(TURNS):
             h = (low + turn) % TURNS
-            term = acc[h, 0, low : low + 256, :] + acc[h, 1, low + 4 : low + 260, :]
+            term = acc[ch, h, 0, low : low + 256, :] + acc[ch, h, 1, low + 4 : low + 260, :]
             mixed = term if mixed is None else jnp.where(group == low, term, mixed)
         if turn:
             mixed = pltpu.roll(mixed, SHIFTS * turn, 1)
@@ -150,11 +160,14 @@
             src_ref=send.at[aligned(peer, 32), :],
             dst_ref=recv.at[aligned(me, 32), :],
             send_sem=sent_in,
-            recv_sem=come_in,
+            recv_sem=come_in.at[me // 8],
             device_id={"wide": peer},
             device_id_type=MESH,
         ).start()
-    recv[aligned(me, 32), :] = send[aligned(me, 32), :]
+    own = pltpu.make_async_copy(
+        send.at[aligned(me, 32), :], recv.at[aligned(me, 32), :], come_in.at[me // 8]
+    )
+    own.start()
 
     fetches[2].wait()
     fetches[3].wait()
@@ -178,16 +191,26 @@
         power = jnp.where(lane_big % 64 < 32, power, block_at * power)
         coarse[:, 64 * ch : 64 * ch + 64] = power[:, 64 * ch : 64 * ch + 64]
 
-    wait_rows(recv, 32 * (PEERS - 1), come_in)
-    for ch in range(2):
-        rows = recv[...].astype(F32).reshape(PEERS, 32, LANES)
-        signal[ch] = rows[:, 8 * ch : 8 * ch + 8].reshape(256, LANES)
-        grad[ch, 0:256] = rows[:, 8 * ch + 16 : 8 * ch + 24].reshape(256, LANES)
-        grad[ch, 256:] = jnp.zeros((16, LANES), F32)
-        build_shifted(ch, grad, shifted)
-
-    for ch in range(2):
-        lags = correlate(ch, signal, shifted, acc, scale)
+    grad[:, 256:] = jnp.zeros((2, 16, LANES), F32)
+    acc[:, :, :, 256:] = jnp.zeros((2, TURNS, 2, 8, LANES), F32)
+    now = [None, None]
+    for plane in range(3, -1, -1):
+        wait_rows(recv, 256, come_in.at[plane])
+        rows = recv[256 * plane : 256 * plane + 256].astype(F32).reshape(8, 32, LANES)
+        for ch in range(2):
+            span = slice(64 * plane, 64 * plane + 64)
+            signal[ch, span] = rows[:, 8 * ch : 8 * ch + 8].reshape(64, LANES)
+            grad[ch, span] = rows[:, 8 * ch + 16 : 8 * ch + 24].reshape(64, LANES)
+            build_shifted(ch, plane, grad, shifted)
+        for ch in range(2):
+            if plane == 3:
+                now[ch] = turned(ch, 255, signal)
+            last = 15 if plane == 3 else 4 * plane + 4
+            for i in range(last, 4 * plane if plane else -1, -1):
+                now[ch] = add_chunk(ch, i, signal, shifted, acc, now[ch])
+
+    for ch in range(2):
+        lags = regroup_lags(ch, acc, scale)
         send_c[:, 8 * ch : 8 * ch + 8, :] = lags.reshape(PEERS, 8, LANES)
     for peer in peers:
         pltpu.make_async_remote_copy(
@@ -271,14 +294,14 @@
             pltpu.VMEM((2, 256, LANES), F32),
             pltpu.VMEM((2, 272, LANES), F32),
             pltpu.VMEM((2, 1024, 256), BF16),
-            pltpu.VMEM((TURNS, 2, 264, LANES), F32),
+            pltpu.VMEM((2, TURNS, 2, 264, LANES), F32),
             pltpu.VMEM((PEERS, 16, LANES), F32),
             pltpu.VMEM((2, 3, LANES, LANES), BF16),
             pltpu.VMEM((256, LANES), F32),
             pltpu.VMEM((1, LANES), F32),
             dma((4,)),
             dma,
-            dma,
+            dma((4,)),
             dma,
             dma,
             dma,

time: 24.4 us -> 24.1 us (0.988)
  Pallas kernels: 23.6 us -> 23.3 us
    pallas_call x1, Pallas kernels: 22.7 us -> 22.4 us  [local(): pl.pallas_call(exchange, out_shape=(jax.ShapeDtypeStruct((PEERS, 16, LANE...]
where the time goes in v6:
time: 24.1 us; the launch traced here: 24 us
  Pallas kernels  23.3 us (97%)
  between operations  0.64 us (3%)
    pallas_call x1, Pallas kernels, local(): pl.pallas_call(exchange, out_shape=(jax.ShapeDtypeStruct((PEERS, 16, LANE...  22.4 us
    pallas_call x1, Pallas kernels, local(): pl.pallas_call(regroup, out_shape=(jax.ShapeDtypeStruct((chans, block), F...  0.94 us

profile of v6, /device:TPU:1, one launch (start us, length us, event | category | flops | bytes accessed | tf_op | source)
XLA Modules:
  0.0 24.0 jit_solution(6200012343432661668)
XLA Ops:
  0.6 22.4 %shard_map.67 = (f32[32,16,128]{2,1,0:T(8,128)S(1)}, f32[32,1,128]{2,1,0:T(1,128)S(1)}) custom-call(bf16[64,1024]{1,0:T(8,128)(2,1)} %x_hbm.1, bf16[64,1024]{1,0:T(8,128)(2,1)} %g_hbm.1, f32[16,64]{1,0:T(8,128)} %bitcast.4, f32[16,64]{1,0:T(8,128)} %bitcast.5), custom_call_target="tpu_custom_call" | custom-call | tf_op jit(solution)/shard_map/pallas_call | solution.py:278
  23.0 0.9 %shard_map.68 = (f32[64,1024]{1,0:T(8,128)}, f32[16,64]{1,0:T(8,128)}, f32[16,64]{1,0:T(8,128)}) custom-call(f32[32,16,128]{2,1,0:T(8,128)S(1)} %get-tuple-element.8.c_ref, f32[32,1,128]{2,1,0:T(1,128)S(1)} %get-tuple-element.9.m_ref), custom_call_target="tpu_custom_call" | custom-call | tf_op jit(solution)/shard_map/pallas_call | solution.py:314

commit v7 on v6

--- a/solution.py
+++ b/solution.py
@@ -15,6 +15,7 @@
 SHIFTS = 32
 TURNS = LANES // SHIFTS
 PEERS = 32
+DISTANT = 10
 RING = (0, 1, 2, 1)
 OFFSETS = sorted(
     ((dz, dy, dc) for dz in range(4) for dy in range(4) for dc in range(2) if dz or dy or dc),
@@ -127,10 +128,10 @@
 
 
 def exchange(
-    x_hbm, g_hbm, res_hbm, dec_hbm, recv_c, recv_m,
+    x_hbm, g_hbm, res_hbm, dec_hbm, recv_c,
     x_ref, g_ref, res_ref, dec_ref, stage, send, recv, signal, grad, shifted,
-    acc, send_c, fine, coarse, send_m,
-    fetched, sent_in, come_in, sent_c, come_c, sent_m, come_m,
+    acc, send_c, fine, coarse,
+    fetched, sent_in, come_in, sent_c, come_c,
 ):
     me = lax.axis_index("wide")
     at = place(me)
@@ -212,16 +213,18 @@
     for ch in range(2):
         lags = regroup_lags(ch, acc, scale)
         send_c[:, 8 * ch : 8 * ch + 8, :] = lags.reshape(PEERS, 8, LANES)
-    for peer in peers:
+    def reply(peer, rows):
         pltpu.make_async_remote_copy(
-            src_ref=send_c.at[peer],
-            dst_ref=recv_c.at[me],
+            src_ref=send_c.at[peer, rows, :],
+            dst_ref=recv_c.at[me, rows, :],
             send_sem=sent_c,
             recv_sem=come_c,
             device_id={"wide": peer},
             device_id_type=MESH,
         ).start()
-    recv_c[me] = send_c[me]
+
+    for peer in peers[:DISTANT]:
+        reply(peer, slice(0, 16))
 
     parts = []
     for ch in range(2):
@@ -238,33 +241,26 @@
     lane = lax.broadcasted_iota(jnp.int32, (1, LANES), 1)
     factor = jnp.where(lane < 64, factors[0], factors[1])
     line = jnp.where(lane % 64 < 16, scale * sums, factor * both)
-    send_m[...] = line
-    recv_m[me] = line
-
-    for peer in peers:
-        pltpu.make_async_remote_copy(
-            src_ref=send_m,
-            dst_ref=recv_m.at[me],
-            send_sem=sent_m,
-            recv_sem=come_m,
-            device_id={"wide": peer},
-            device_id_type=MESH,
-        ).start()
+    send_c[:, 16:17, :] = jnp.broadcast_to(line[None], (PEERS, 1, LANES))
+    for peer in peers[:DISTANT]:
+        reply(peer, slice(16, 17))
+    for peer in peers[DISTANT:]:
+        reply(peer, slice(0, 17))
+    recv_c[me] = send_c[me]
 
     wait_rows(send, 32 * (PEERS - 1), sent_in)
-    wait_rows(send_c, PEERS - 1, sent_c)
-    wait_rows(recv_m, PEERS - 1, sent_m)
-    wait_rows(recv_c, PEERS - 1, come_c)
-    wait_rows(recv_m, PEERS - 1, come_m)
-
-
-def regroup(c_ref, m_ref, out_ref, rg_ref, ld_ref):
+    part = send_c.at[0 : PEERS - 1, 0:17, :]
+    pltpu.make_async_copy(part, part, sent_c).wait()
+    pltpu.make_async_copy(part, part, come_c).wait()
+
+
+def regroup(c_ref, out_ref, rg_ref, ld_ref):
     for ch in range(2):
         for k in range(8):
             out_ref[PEERS * ch : PEERS * (ch + 1), k * LANES : (k + 1) * LANES] = c_ref[
                 :, 8 * ch + k, :
             ]
-    lines = jnp.transpose(m_ref[:, 0, :])
+    lines = jnp.transpose(c_ref[:, 16, :])
     rg_ref[...] = jnp.concatenate([lines[0:16], lines[64:80]], axis=1)
     ld_ref[...] = jnp.concatenate([lines[16:32], lines[80:96]], axis=1)
 
@@ -275,14 +271,11 @@
     vmem = pl.BlockSpec(memory_space=pltpu.VMEM)
     hbm = pl.BlockSpec(memory_space=pltpu.HBM)
     dma = pltpu.SemaphoreType.DMA
-    lags, lines = pl.pallas_call(
+    replies = pl.pallas_call(
         exchange,
-        out_shape=(
-            jax.ShapeDtypeStruct((PEERS, 16, LANES), F32),
-            jax.ShapeDtypeStruct((PEERS, 1, LANES), F32),
-        ),
+        out_shape=jax.ShapeDtypeStruct((PEERS, 24, LANES), F32),
         in_specs=[hbm] * 4,
-        out_specs=(vmem, vmem),
+        out_specs=vmem,
         scratch_shapes=[
             pltpu.VMEM((chans, block), BF16),
             pltpu.VMEM((chans, block), BF16),
@@ -295,15 +288,12 @@
             pltpu.VMEM((2, 272, LANES), F32),
             pltpu.VMEM((2, 1024, 256), BF16),
             pltpu.VMEM((2, TURNS, 2, 264, LANES), F32),
-            pltpu.VMEM((PEERS, 16, LANES), F32),
+            pltpu.VMEM((PEERS, 24, LANES), F32),
             pltpu.VMEM((2, 3, LANES, LANES), BF16),
             pltpu.VMEM((256, LANES), F32),
-            pltpu.VMEM((1, LANES), F32),
             dma((4,)),
             dma,
             dma((4,)),
-            dma,
-            dma,
             dma,
             dma,
         ],
@@ -318,10 +308,10 @@
             jax.ShapeDtypeStruct((modes, chans), F32),
             jax.ShapeDtypeStruct((modes, chans), F32),
         ),
-        in_specs=[vmem] * 2,
+        in_specs=[vmem],
         out_specs=(vmem,) * 3,
         compiler_params=pltpu.CompilerParams(vmem_limit_bytes=4 * 2**20),
-    )(lags, lines)
+    )(replies)
     return filter_grad, residue_grad.T, log_decay_grad.T
 
 

time: 24.1 us -> 23.3 us (0.967)
  Pallas kernels: 23.3 us -> 22.5 us
    pallas_call x1, Pallas kernels: 22.4 us -> 21.6 us  [local(): pl.pallas_call(exchange, out_shape=jax.ShapeDtypeStruct((PEERS, 24, LANES...]
where the time goes in v7:
time: 23.3 us; the launch traced here: 23.2 us
  Pallas kernels  22.5 us (97%)
  between operations  0.64 us (3%)
    pallas_call x1, Pallas kernels, local(): pl.pallas_call(exchange, out_shape=jax.ShapeDtypeStruct((PEERS, 24, LANES...  21.6 us
    pallas_call x1, Pallas kernels, local(): pl.pallas_call(regroup, out_shape=(jax.ShapeDtypeStruct((chans, block), F...  0.94 us

profile of v7, /device:TPU:1, one launch (start us, length us, event | category | flops | bytes accessed | tf_op | source)
XLA Modules:
  0.0 23.2 jit_solution(14059928005795388481)
XLA Ops:
  0.6 21.6 %shard_map.67.c_ref = f32[32,24,128]{2,1,0:T(8,128)S(1)} custom-call(bf16[64,1024]{1,0:T(8,128)(2,1)} %x_hbm.1, bf16[64,1024]{1,0:T(8,128)(2,1)} %g_hbm.1, f32[16,64]{1,0:T(8,128)} %bitcast.4, f32[16,64]{1,0:T(8,128)} %bitcast.5), custom_call_target="tpu_custom_call" | custom-call | tf_op jit(solution)/shard_map/pallas_call | solution.py:274
  22.2 0.9 %shard_map.68 = (f32[64,1024]{1,0:T(8,128)}, f32[16,64]{1,0:T(8,128)}, f32[16,64]{1,0:T(8,128)}) custom-call(f32[32,24,128]{2,1,0:T(8,128)S(1)} %shard_map.67.c_ref), custom_call_target="tpu_custom_call" | custom-call | tf_op jit(solution)/shard_map/pallas_call | solution.py:304

commit v8 on v7

--- a/solution.py
+++ b/solution.py
@@ -9,12 +9,14 @@
 
 F32 = jnp.float32
 BF16 = jnp.bfloat16
+PAIRS = ((0, 0), (0, 1), (1, 0), (1, 1), (0, 2), (2, 0))
 MESH = pl.DeviceIdType.MESH
 
 LANES = 128
 SHIFTS = 32
 TURNS = LANES // SHIFTS
 PEERS = 32
+GROUPS = ((24, 8), (16, 8), (12, 4), (0, 12))
 DISTANT = 10
 RING = (0, 1, 2, 1)
 OFFSETS = sorted(
@@ -68,19 +70,19 @@
     return jnp.concatenate(halves, axis=1), now
 
 
-def build_shifted(ch, plane, grad, shifted):
-    first = 64 * plane
-    lane = lax.broadcasted_iota(jnp.int32, (72, LANES), 1)
-    here = grad[ch, first : first + 72, :]
-    after = grad[ch, first + 1 : first + 73, :]
+def build_shifted(ch, first, count, grad, shifted):
+    lane = lax.broadcasted_iota(jnp.int32, (count + 8, LANES), 1)
+    here = grad[ch, first : first + count + 8, :]
+    after = grad[ch, first + 1 : first + count + 9, :]
     turns = []
     for h in range(TURNS):
         moved = here
         if h:
             moved = pltpu.roll(jnp.where(lane < SHIFTS * h, after, here), LANES - SHIFTS * h, 1)
-        turns.append(jnp.concatenate([moved[0:64], moved[8:72]], axis=1).reshape(8, 8, 256))
-    shifted[ch, 4 * first : 4 * first + 256] = (
-        jnp.stack(turns, axis=1).reshape(256, 256).astype(BF16)
+        both = jnp.concatenate([moved[0:count], moved[8 : count + 8]], axis=1)
+        turns.append(both.reshape(count // 8, 8, 256))
+    shifted[ch, 4 * first : 4 * first + 4 * count] = (
+        jnp.stack(turns, axis=1).reshape(4 * count, 256).astype(BF16)
     )
 
 
@@ -127,6 +129,15 @@
     return jnp.sum(jnp.where(lane % 16 == sub, spread, 0.0), axis=0, keepdims=True)
 
 
+def split(values):
+    parts = []
+    for _ in range(3):
+        part = values.astype(BF16)
+        parts.append(part)
+        values = values - part.astype(F32)
+    return parts
+
+
 def exchange(
     x_hbm, g_hbm, res_hbm, dec_hbm, recv_c,
     x_ref, g_ref, res_ref, dec_ref, stage, send, recv, signal, grad, shifted,
@@ -156,17 +167,20 @@
     send[...] = stage[...].astype(BF16)
     pl.semaphore_wait(barrier, PEERS - 1)
 
+    group = len(GROUPS) - 1
+    for n in range(len(GROUPS) - 2, -1, -1):
+        group = jnp.where(me >= GROUPS[n][0], n, group)
     for peer in peers:
         pltpu.make_async_remote_copy(
             src_ref=send.at[aligned(peer, 32), :],
             dst_ref=recv.at[aligned(me, 32), :],
             send_sem=sent_in,
-            recv_sem=come_in.at[me // 8],
+            recv_sem=come_in.at[group],
             device_id={"wide": peer},
             device_id_type=MESH,
         ).start()
     own = pltpu.make_async_copy(
-        send.at[aligned(me, 32), :], recv.at[aligned(me, 32), :], come_in.at[me // 8]
+        send.at[aligned(me, 32), :], recv.at[aligned(me, 32), :], come_in.at[group]
     )
     own.start()
 
@@ -184,10 +198,9 @@
         power = jnp.where(own, jnp.exp(-rate * offset_at), 0.0)
         weighted = jnp.logical_and(lane_small % 64 >= 16, lane_small % 64 < 32)
         power = jnp.where(weighted, offset_at * power, power)
-        upper = power.astype(BF16)
-        fine[ch, 0] = upper
-        fine[ch, 1] = upper
-        fine[ch, 2] = (power - upper.astype(F32)).astype(BF16)
+        thirds = split(power)
+        for n, (_, which) in enumerate(PAIRS):
+            fine[ch, n] = thirds[which]
         power = jnp.exp(-rate * block_at)
         power = jnp.where(lane_big % 64 < 32, power, block_at * power)
         coarse[:, 64 * ch : 64 * ch + 64] = power[:, 64 * ch : 64 * ch + 64]
@@ -195,24 +208,32 @@
     grad[:, 256:] = jnp.zeros((2, 16, LANES), F32)
     acc[:, :, :, 256:] = jnp.zeros((2, TURNS, 2, 8, LANES), F32)
     now = [None, None]
-    for plane in range(3, -1, -1):
-        wait_rows(recv, 256, come_in.at[plane])
-        rows = recv[256 * plane : 256 * plane + 256].astype(F32).reshape(8, 32, LANES)
+    last = 15
+    for n, (first, count) in enumerate(GROUPS):
+        wait_rows(recv, 32 * count, come_in.at[n])
+        rows = recv[32 * first : 32 * (first + count)].astype(F32).reshape(count, 32, LANES)
         for ch in range(2):
-            span = slice(64 * plane, 64 * plane + 64)
-            signal[ch, span] = rows[:, 8 * ch : 8 * ch + 8].reshape(64, LANES)
-            grad[ch, span] = rows[:, 8 * ch + 16 : 8 * ch + 24].reshape(64, LANES)
-            build_shifted(ch, plane, grad, shifted)
+            span = slice(8 * first, 8 * (first + count))
+            signal[ch, span] = rows[:, 8 * ch : 8 * ch + 8].reshape(8 * count, LANES)
+            grad[ch, span] = rows[:, 8 * ch + 16 : 8 * ch + 24].reshape(8 * count, LANES)
+        least = first // 2 + 1 if first else 0
         for ch in range(2):
-            if plane == 3:
+            if n == 0:
                 now[ch] = turned(ch, 255, signal)
-            last = 15 if plane == 3 else 4 * plane + 4
-            for i in range(last, 4 * plane if plane else -1, -1):
+            else:
+                now[ch] = add_chunk(ch, last, signal, shifted, acc, now[ch])
+        for ch in range(2):
+            build_shifted(ch, 8 * first, 8 * count, grad, shifted)
+        if n:
+            last -= 1
+        for ch in range(2):
+            for i in range(last, least - 1, -1):
                 now[ch] = add_chunk(ch, i, signal, shifted, acc, now[ch])
-
-    for ch in range(2):
-        lags = regroup_lags(ch, acc, scale)
-        send_c[:, 8 * ch : 8 * ch + 8, :] = lags.reshape(PEERS, 8, LANES)
+            if first == 0:
+                lags = regroup_lags(ch, acc, scale)
+                send_c[:, 8 * ch : 8 * ch + 8, :] = lags.reshape(PEERS, 8, LANES)
+        last = least - 1
+
     def reply(peer, rows):
         pltpu.make_async_remote_copy(
             src_ref=send_c.at[peer, rows, :],
@@ -229,11 +250,11 @@
     parts = []
     for ch in range(2):
         lags = send_c[:, 8 * ch : 8 * ch + 8, :].reshape(256, LANES)
-        upper = lags.astype(BF16)
-        parts += [upper, (lags - upper.astype(F32)).astype(BF16), upper]
+        thirds = split(lags)
+        parts += [thirds[which] for which, _ in PAIRS]
     mixed = jnp.dot(
         jnp.concatenate(parts, axis=1),
-        fine[...].reshape(6 * LANES, LANES),
+        fine[...].reshape(2 * len(PAIRS) * LANES, LANES),
         preferred_element_type=F32,
     )
     sums = jnp.sum(mixed * coarse[...], axis=0, keepdims=True)
@@ -246,7 +267,7 @@
         reply(peer, slice(16, 17))
     for peer in peers[DISTANT:]:
         reply(peer, slice(0, 17))
-    recv_c[me] = send_c[me]
+    recv_c[me, 0:17] = send_c[me, 0:17]
 
     wait_rows(send, 32 * (PEERS - 1), sent_in)
     part = send_c.at[0 : PEERS - 1, 0:17, :]
@@ -289,11 +310,11 @@
             pltpu.VMEM((2, 1024, 256), BF16),
             pltpu.VMEM((2, TURNS, 2, 264, LANES), F32),
             pltpu.VMEM((PEERS, 24, LANES), F32),
-            pltpu.VMEM((2, 3, LANES, LANES), BF16),
+            pltpu.VMEM((2, len(PAIRS), LANES, LANES), BF16),
             pltpu.VMEM((256, LANES), F32),
             dma((4,)),
             dma,
-            dma((4,)),
+            dma((len(GROUPS),)),
             dma,
             dma,
         ],

time: 23.3 us -> 23.3 us (level)
  no operation moved by 1% of the time
where the time goes in v8:
time: 23.3 us; the launch traced here: 23.1 us
  Pallas kernels  22.5 us (97%)
  between operations  0.64 us (3%)
    pallas_call x1, Pallas kernels, local(): pl.pallas_call(exchange, out_shape=jax.ShapeDtypeStruct((PEERS, 24, LANES...  21.6 us
    pallas_call x1, Pallas kernels, local(): pl.pallas_call(regroup, out_shape=(jax.ShapeDtypeStruct((chans, block), F...  0.94 us

profile of v8, /device:TPU:1, one launch (start us, length us, event | category | flops | bytes accessed | tf_op | source)
XLA Modules:
  0.0 23.1 jit_solution(10238089963066686450)
XLA Ops:
  0.6 21.6 %shard_map.67.c_ref = f32[32,24,128]{2,1,0:T(8,128)S(1)} custom-call(bf16[64,1024]{1,0:T(8,128)(2,1)} %x_hbm.1, bf16[64,1024]{1,0:T(8,128)(2,1)} %g_hbm.1, f32[16,64]{1,0:T(8,128)} %bitcast.4, f32[16,64]{1,0:T(8,128)} %bitcast.5), custom_call_target="tpu_custom_call" | custom-call | tf_op jit(solution)/shard_map/pallas_call | solution.py:295
  22.2 0.9 %shard_map.68 = (f32[64,1024]{1,0:T(8,128)}, f32[16,64]{1,0:T(8,128)}, f32[16,64]{1,0:T(8,128)}) custom-call(f32[32,24,128]{2,1,0:T(8,128)S(1)} %shard_map.67.c_ref), custom_call_target="tpu_custom_call" | custom-call | tf_op jit(solution)/shard_map/pallas_call | solution.py:325

commit v9 on v8

--- a/solution.py
+++ b/solution.py
@@ -139,7 +139,7 @@
 
 
 def exchange(
-    x_hbm, g_hbm, res_hbm, dec_hbm, recv_c,
+    x_hbm, g_hbm, res_hbm, dec_hbm, lags_ref, lines_ref, recv_c,
     x_ref, g_ref, res_ref, dec_ref, stage, send, recv, signal, grad, shifted,
     acc, send_c, fine, coarse,
     fetched, sent_in, come_in, sent_c, come_c,
@@ -239,7 +239,7 @@
             src_ref=send_c.at[peer, rows, :],
             dst_ref=recv_c.at[me, rows, :],
             send_sem=sent_c,
-            recv_sem=come_c,
+            recv_sem=come_c.at[me // 8],
             device_id={"wide": peer},
             device_id_type=MESH,
         ).start()
@@ -267,23 +267,39 @@
         reply(peer, slice(16, 17))
     for peer in peers[DISTANT:]:
         reply(peer, slice(0, 17))
-    recv_c[me, 0:17] = send_c[me, 0:17]
+    own = pltpu.make_async_copy(
+        send_c.at[me, 0:17, :], recv_c.at[me, 0:17, :], come_c.at[me // 8]
+    )
+    own.start()
 
     wait_rows(send, 32 * (PEERS - 1), sent_in)
     part = send_c.at[0 : PEERS - 1, 0:17, :]
     pltpu.make_async_copy(part, part, sent_c).wait()
-    pltpu.make_async_copy(part, part, come_c).wait()
-
-
-def regroup(c_ref, out_ref, rg_ref, ld_ref):
-    for ch in range(2):
-        for k in range(8):
-            out_ref[PEERS * ch : PEERS * (ch + 1), k * LANES : (k + 1) * LANES] = c_ref[
-                :, 8 * ch + k, :
-            ]
-    lines = jnp.transpose(c_ref[:, 16, :])
+    for plane in range(3, -1, -1):
+        part = recv_c.at[8 * plane : 8 * plane + 8, 0:17, :]
+        pltpu.make_async_copy(part, part, come_c.at[plane]).wait()
+        for ch in range(2):
+            for k in range(8):
+                lags_ref[
+                    PEERS * ch + 8 * plane : PEERS * ch + 8 * plane + 8,
+                    k * LANES : (k + 1) * LANES,
+                ] = recv_c[8 * plane : 8 * plane + 8, 8 * ch + k, :]
+        lines_ref[8 * plane : 8 * plane + 8, :] = recv_c[8 * plane : 8 * plane + 8, 16, :]
+
+
+def regroup(lags_ref, lines_ref, out_hbm, rg_hbm, ld_hbm, rg_ref, ld_ref, sems):
+    copies = [
+        pltpu.make_async_copy(src, dst, sems.at[n])
+        for n, (src, dst) in enumerate(((lags_ref, out_hbm), (rg_ref, rg_hbm), (ld_ref, ld_hbm)))
+    ]
+    copies[0].start()
+    lines = jnp.transpose(lines_ref[...])
     rg_ref[...] = jnp.concatenate([lines[0:16], lines[64:80]], axis=1)
+    copies[1].start()
     ld_ref[...] = jnp.concatenate([lines[16:32], lines[80:96]], axis=1)
+    copies[2].start()
+    for copy in copies:
+        copy.wait()
 
 
 def local(inputs, out_grad, residues, decay):
@@ -292,12 +308,16 @@
     vmem = pl.BlockSpec(memory_space=pltpu.VMEM)
     hbm = pl.BlockSpec(memory_space=pltpu.HBM)
     dma = pltpu.SemaphoreType.DMA
-    replies = pl.pallas_call(
+    lags, lines = pl.pallas_call(
         exchange,
-        out_shape=jax.ShapeDtypeStruct((PEERS, 24, LANES), F32),
+        out_shape=(
+            jax.ShapeDtypeStruct((chans, block), F32),
+            jax.ShapeDtypeStruct((PEERS, LANES), F32),
+        ),
         in_specs=[hbm] * 4,
-        out_specs=vmem,
+        out_specs=(vmem, vmem),
         scratch_shapes=[
+            pltpu.VMEM((PEERS, 24, LANES), F32),
             pltpu.VMEM((chans, block), BF16),
             pltpu.VMEM((chans, block), BF16),
             pltpu.VMEM((modes, chans), F32),
@@ -316,7 +336,7 @@
             dma,
             dma((len(GROUPS),)),
             dma,
-            dma,
+            dma((4,)),
         ],
         compiler_params=pltpu.CompilerParams(
             collective_id=0, has_side_effects=True, vmem_limit_bytes=32 * 2**20
@@ -329,10 +349,15 @@
             jax.ShapeDtypeStruct((modes, chans), F32),
             jax.ShapeDtypeStruct((modes, chans), F32),
         ),
-        in_specs=[vmem],
-        out_specs=(vmem,) * 3,
+        in_specs=[vmem] * 2,
+        out_specs=(hbm,) * 3,
+        scratch_shapes=[
+            pltpu.VMEM((modes, chans), F32),
+            pltpu.VMEM((modes, chans), F32),
+            dma((3,)),
+        ],
         compiler_params=pltpu.CompilerParams(vmem_limit_bytes=4 * 2**20),
-    )(replies)
+    )(lags, lines)
     return filter_grad, residue_grad.T, log_decay_grad.T
 
 

time: 23.3 us -> 23.3 us (level)
  no operation moved by 1% of the time
where the time goes in v9:
time: 23.3 us; the launch traced here: 23.1 us
  Pallas kernels  22.5 us (97%)
  between operations  0.64 us (3%)
    pallas_call x1, Pallas kernels, local(): pl.pallas_call(exchange, out_shape=(jax.ShapeDtypeStruct((chans, block),...  21.7 us
    pallas_call x1, Pallas kernels, local(): pl.pallas_call(regroup, out_shape=(jax.ShapeDtypeStruct((chans, block), F...  0.79 us

profile of v9, /device:TPU:1, one launch (start us, length us, event | category | flops | bytes accessed | tf_op | source)
XLA Modules:
  0.0 23.1 jit_solution(11702740792602020809)
XLA Ops:
  0.6 21.7 %shard_map.67 = (f32[64,1024]{1,0:T(8,128)S(1)}, f32[32,128]{1,0:T(8,128)S(1)}) custom-call(bf16[64,1024]{1,0:T(8,128)(2,1)} %x_hbm.1, bf16[64,1024]{1,0:T(8,128)(2,1)} %g_hbm.1, f32[16,64]{1,0:T(8,128)} %bitcast.4, f32[16,64]{1,0:T(8,128)} %bitcast.5), custom_call_target="tpu_custom_call" | custom-call | tf_op jit(solution)/shard_map/pallas_call | solution.py:311
  22.3 0.8 %shard_map.68 = (f32[64,1024]{1,0:T(8,128)}, f32[16,64]{1,0:T(8,128)}, f32[16,64]{1,0:T(8,128)}) custom-call(f32[64,1024]{1,0:T(8,128)S(1)} %get-tuple-element.8.lags_ref, f32[32,128]{1,0:T(8,128)S(1)} %get-tuple-element.9.lines_ref), custom_call_target="tpu_custom_call" | custom-call | tf_op jit(solution)/shard_map/pallas_call | solution.py:345
